TPU v7x, 256 devices: a whole 4x4x8 slice. The times are simulated.
256 devices in a mesh: fsdp: 64 (over z, y, core), group: 4 (over x).
Axes of the slice: x: 4, y: 4, z: 8, core: 2. Of those that a mesh axis runs over, the one named last changes fastest.
Arguments:
- grads: bfloat16 [56, 1024, 1024], P(None, 'fsdp', 'group'), may hold values from -0.29882812 to 0.29882812
- second_moment: float32 [56, 1024, 1024], P(None, 'fsdp', 'group'), may hold values from 0.0001 to 0.01
- slot_of: int32 [56], replicated, may hold values from 0 to 127, as said below
- block_rows: int32 [56], replicated, may hold values from 512 to 1024
- block_cols: int32 [56], replicated, may hold values from 512 to 1024
- left_stat: float32 [128, 1024, 1024], P('fsdp', 'group')
- right_stat: float32 [128, 1024, 1024], P('fsdp', 'group')
- left_root: bfloat16 [128, 1024, 1024], P('fsdp', 'group'), as said below
- right_root: bfloat16 [128, 1024, 1024], P('fsdp', None, 'group'), as said below
Outputs:
- directions: bfloat16 [56, 1024, 1024], P(None, 'fsdp', 'group')
- new_moment: float32 [56, 1024, 1024], P(None, 'fsdp', 'group')
- new_left: float32 [128, 1024, 1024], P('fsdp', 'group')
- new_right: float32 [128, 1024, 1024], P('fsdp', 'group')
Inputs may be any that keep to these rules, and one draw needn't show every extreme that they name: slot_of holds distinct values; every owner (value // 2) receives at most 2 blocks, owner 0 receives exactly 2, and slot 127 always holds a block. `left_root`: each matrix is symmetric. `right_root`: each matrix is symmetric.
All inputs are finite; a program needn't handle non-finite values.
Results may differ from a plain program's by a relative error of at most 0.005.
Values may be sent and summed in bfloat16 or wider, within the bound.
A program may use at most 64 MiB of HBM per device.

v0:
```python
import jax
import jax.numpy as jnp
from jax import lax
from jax.sharding import PartitionSpec as P


def local(
    grads,
    second_moment,
    slot_of,
    block_rows,
    block_cols,
    left_stat,
    right_stat,
    left_root,
    right_root,
):
    nblocks, rows_here, cols_here = grads.shape
    fsdp_count = lax.axis_size("fsdp")
    slots = left_stat.shape[0]
    edge = left_root.shape[2]
    quarter = right_root.shape[2]
    group_at = lax.axis_index("group")
    owner_at = lax.axis_index("fsdp")
    row_index = owner_at * rows_here + jnp.arange(rows_here, dtype=jnp.int32)
    col_index = group_at * cols_here + jnp.arange(cols_here, dtype=jnp.int32)
    mask = (row_index[None, :, None] < block_rows[:, None, None]) & (
        col_index[None, None, :] < block_cols[:, None, None]
    )
    grad = jnp.where(mask, grads, jnp.zeros_like(grads))
    grad32 = grad.astype(jnp.float32)
    moment = 0.95 * second_moment + 0.05 * grad32 * grad32
    adam = grad32 / (jnp.sqrt(moment) + 1e-08)
    adam_sq = lax.psum(jnp.sum(adam * adam, axis=(1, 2)), ("fsdp", "group"))
    total_slots = fsdp_count * slots
    match = slot_of[None, :] == jnp.arange(total_slots, dtype=jnp.int32)[:, None]
    filled = jnp.any(match, axis=1)
    source = jnp.sum(jnp.where(match, jnp.arange(nblocks, dtype=jnp.int32)[None, :], 0), axis=1)
    in_slots = jnp.where(
        filled[:, None, None], jnp.take(grad, source, axis=0), jnp.zeros((), grad.dtype)
    )
    wide = lax.all_gather(in_slots, "group", axis=2, tiled=True)
    full = lax.all_to_all(wide, "fsdp", split_axis=0, concat_axis=1, tiled=True)
    mine = lax.dynamic_slice_in_dim(match, owner_at * slots, slots, 0)
    rows_mine = jnp.sum(jnp.where(mine, block_rows[None, :], 0), axis=1)
    cols_mine = jnp.sum(jnp.where(mine, block_cols[None, :], 0), axis=1)
    adam_mine = jnp.sum(jnp.where(mine, adam_sq[None, :], 0.0), axis=1)
    row_block = lax.dynamic_slice_in_dim(full, group_at * quarter, quarter, 1)
    col_block = lax.dynamic_slice_in_dim(full, group_at * quarter, quarter, 2)
    gram_left = jnp.einsum("sik,sjk->sij", row_block, full, preferred_element_type=jnp.float32)
    gram_right = jnp.einsum("ski,skj->sij", col_block, full, preferred_element_type=jnp.float32)
    new_left = 0.9 * left_stat + 0.1 * gram_left
    new_right = 0.9 * right_stat + 0.1 * gram_right
    mixed = jnp.einsum("sik,skj->sij", full, right_root, preferred_element_type=jnp.float32).astype(
        jnp.bfloat16
    )
    precond = jnp.einsum(
        "ski,skj->sij",
        lax.all_gather(left_root, "group", axis=1, tiled=True),
        mixed,
        preferred_element_type=jnp.float32,
    )
    out_rows = jnp.arange(edge, dtype=jnp.int32)
    out_cols = group_at * quarter + jnp.arange(quarter, dtype=jnp.int32)
    keep = (out_rows[None, :, None] < rows_mine[:, None, None]) & (
        out_cols[None, None, :] < cols_mine[:, None, None]
    )
    precond = jnp.where(keep, precond, jnp.float32(0.0))
    precond_sq = lax.psum(jnp.sum(precond * precond, axis=(1, 2)), "group")
    factor = jnp.sqrt(adam_mine) / (jnp.sqrt(precond_sq) + 1e-06)
    direction = (precond * factor[:, None, None]).astype(jnp.bfloat16)
    returned = lax.all_to_all(direction, "fsdp", split_axis=1, concat_axis=0, tiled=True)
    directions = jnp.take(returned, slot_of, axis=0)
    return (directions, moment, new_left, new_right)


def solution(mesh):
    placed = (
        P(None, "fsdp", "group"),
        P(None, "fsdp", "group"),
        P(),
        P(),
        P(),
        P("fsdp", "group", None),
        P("fsdp", "group", None),
        P("fsdp", "group", None),
        P("fsdp", None, "group"),
    )
    return jax.shard_map(
        local,
        mesh=mesh,
        in_specs=placed,
        out_specs=(
            P(None, "fsdp", "group"),
            P(None, "fsdp", "group"),
            P("fsdp", "group", None),
            P("fsdp", "group", None),
        ),
        check_vma=False,
    )
```

profile of v0, /device:TPU:1, one launch (start us, length us, event | category | flops | bytes accessed | tf_op | source)
XLA Modules:
  0.0 293.0 jit_solution(12755377168922969836)
XLA Ops:
  7.2 0.0 copy-start
  7.2 0.0 all-gather.3.cloned.1.call-start
  7.2 0.8 iota_compare_fusion
  8.1 0.8 select_reduce_fusion
  8.9 0.7 broadcast_compare_fusion
  9.7 0.7 broadcast_compare_fusion.1
  10.4 3.1 %fusion.4 = (f32[56]{0:T(128)S(1)}, f32[56,16,256]{2,1,0:T(8,128)}, bf16[56,16,256]{2,1,0:T(8,128)(2,1)S(1)}) fusion(f32[56,16,256]{2,1,0:T(8,128)} %param.10, bf16[56,16,256]{2,1,0:T(8,128)(2,1)} %param.9, pred[56,256]{1,0:T(8,128)(4,1)S(1)} %broadcast_compare_fusion, pred[56,16]{1,0:T(8,128)(4,1)S(1)} %broadcast_compare_fusion.1), kind=kLoop, calls=%fused_computation.15 | loop fusion | flops 2523080 | bytes 2767968 | tf_op jit(solution)/shard_map/reduce_sum | solution.py:34
  13.5 0.6 gather_fusion
  14.2 1.5 select_select_fusion
  15.7 0.0 all-gather.3.cloned.1.call-update
  15.7 0.0 copy-start.3
  15.7 0.0 copy-start.4
  15.7 57.6 %all-gather.3.cloned.1.call-done = bf16[128,16,1024]{2,1,0:T(8,128)(2,1)} async-done(((bf16[128,16,256]{2,1,0:T(8,128)(2,1)}), bf16[128,16,1024]{2,1,0:T(8,128)(2,1)}) %all-gather.3.cloned.1.call-update) | async-done | bytes 4194320 | tf_op jit(solution)/shard_map/all_gather | solution.py:42
  73.3 11.7 %all-to-all-start = ((bf16[128,16,1024]{2,1,0:T(8,128)(2,1)}), bf16[128,16,1024]{2,1,0:T(8,128)(2,1)}, u32[]{:S(2)}, u32[]{:S(2)}) async-start(bf16[128,16,1024]{2,1,0:T(8,128)(2,1)} %all-gather.3.cloned.1.call-done), calls=%async_computation | async-start | bytes 8388608 | tf_op jit(solution)/shard_map/all_to_all | solution.py:43
  85.1 0.0 all-gather.5.cloned.1.call-start
  85.1 0.7 all-gather.5.cloned.1.call-update
  85.8 136.3 %psum.14 = f32[56]{0:T(128)S(1)} all-reduce(f32[56]{0:T(128)S(1)} %get-tuple-element.6), channel_id=1, replica_groups=mesh['fsdp'=64,'group'=4] {'fsdp','group'}, use_global_device_ids=true, to_apply=%region_5.6 | all-reduce | flops 56 | bytes 448 | tf_op jit(solution)/shard_map/psum | solution.py:34
  222.1 0.1 select_reduce_fusion.1
  222.3 0.0 copy-done.3
  222.3 0.0 copy-done.4
  222.3 0.2 select_reduce_fusion.3
  222.4 0.1 broadcast_compare_fusion.2
  222.5 0.1 iota_compare_fusion.1
  222.6 0.0 all-to-all-done
  222.6 5.0 %copy.27 = bf16[64,2,16,1024]{3,2,0,1:T(8,128)(2,1)} copy(bf16[64,2,16,1024]{3,2,1,0:T(8,128)(2,1)} %bitcast.2) | data formatting | bytes 8388608 | tf_op jit(solution)/shard_map/all_to_all | solution.py:43
  227.6 0.0 all-gather.5.cloned.1.call-done
  227.6 0.0 copy-done
  227.6 7.1 %multiply_reduce_fusion = (f32[2]{0:T(128)S(1)}, f32[2,256,1024]{2,1,0:T(8,128)}) fusion(pred[2,256]{1,0:T(4,128)(4,1)S(1)} %broadcast_compare_fusion.2, pred[2,1024]{1,0:T(4,128)(4,1)S(1)} %iota_compare_fusion.1, bf16[2,1024,1024]{2,1,0:T(8,128)(2,1)} %all-gather.5.cloned.1.call-done, bf16[2,1024,1024]{2,1,0:T(8,128)(2,1)} %bitcast.23, ...), kind=kOutput, calls=%fused_computation.6 | convolution fusion | flops 2150105088 | bytes 11536904 | tf_op jit(solution)/shard_map/ski,skj->sij/dot_general | solution.py:57
  234.7 7.7 %psum.15 = f32[2]{0:T(128)S(1)} all-reduce(f32[2]{0:T(128)S(1)} %get-tuple-element.11), channel_id=1, replica_groups=mesh['fsdp'=64,'group'=4] {'group'}, use_global_device_ids=true, to_apply=%region_8.9 | all-reduce | flops 2 | bytes 16 | tf_op jit(solution)/shard_map/psum | solution.py:69
  242.5 2.0 multiply_convert_fusion
  244.5 0.0 copy-start.5
  244.5 2.0 copy.29
  246.5 9.8 %all-to-all-start.1 = ((bf16[2,1024,256]{2,0,1:T(2,128)(2,1)}), bf16[2,1024,256]{2,0,1:T(2,128)(2,1)S(1)}, u32[]{:S(2)}, u32[]{:S(2)}) async-start(bf16[2,1024,256]{2,0,1:T(2,128)(2,1)} %copy.29), calls=%async_computation.1 | async-start | bytes 2097152 | tf_op jit(solution)/shard_map/all_to_all | solution.py:72
  256.4 0.0 copy-done.5
  256.4 0.0 copy-start.1
  256.4 0.0 copy-start.2
  256.4 6.1 %multiply_add_fusion = f32[2,256,1024]{2,1,0:T(8,128)} fusion(f32[2,256,1024]{2,1,0:T(8,128)} %param.15, bf16[2,1024,1024]{2,1,0:T(8,128)(2,1)} %bitcast.24, s32[]{:T(128)S(6)} %select_n.76), kind=kOutput, calls=%fused_computation.3 | convolution fusion | flops 1075314688 | bytes 9437188 | tf_op jit(solution)/shard_map/ski,skj->sij/dot_general | solution.py:51
  262.5 0.0 copy-done.1
  262.5 0.0 copy-done.2
  262.5 2.8 multiply_add_fusion.1
  265.3 19.1 %all-to-all-done.1 = bf16[2,1024,256]{2,0,1:T(2,128)(2,1)S(1)} async-done(((bf16[2,1024,256]{2,0,1:T(2,128)(2,1)}), bf16[2,1024,256]{2,0,1:T(2,128)(2,1)S(1)}, u32[]{:S(2)}, u32[]{:S(2)}) %all-to-all-start.1) | async-done | bytes 1048608 | tf_op jit(solution)/shard_map/all_to_all | solution.py:72
  284.3 0.1 copy.30
  284.5 0.1 copy.31
  284.6 0.6 gather_fusion.1
  285.2 0.9 broadcast_select_fusion
  (9 shorter events, 0.1 us)
Async XLA Ops:
  7.2 220.4 %copy-start = (bf16[2,1024,256]{2,1,0:T(8,128)(2,1)S(1)}, bf16[2,1024,256]{2,1,0:T(8,128)(2,1)}, u32[]{:S(2)}) copy-start(bf16[2,1024,256]{2,1,0:T(8,128)(2,1)} %param.17) | copy-start | bytes 3145732
  7.2 66.1 %all-gather.3.cloned.1.call-start = ((), (), s32[]{:S(2)}) async-start(), calls=%async_computation.2 | async-start | bytes 5242880 | tf_op jit(solution)/shard_map/all_gather | solution.py:42
  15.7 206.6 %copy-start.3 = (s32[56]{0:T(128)S(1)}, s32[56]{0:T(128)}, u32[]{:S(2)}) copy-start(s32[56]{0:T(128)} %param.12) | copy-start | bytes 676
  15.7 206.6 %copy-start.4 = (s32[56]{0:T(128)S(1)}, s32[56]{0:T(128)}, u32[]{:S(2)}) copy-start(s32[56]{0:T(128)} %param.13) | copy-start | bytes 676
  73.3 149.3 %all-to-all-start = ((bf16[128,16,1024]{2,1,0:T(8,128)(2,1)}), bf16[128,16,1024]{2,1,0:T(8,128)(2,1)}, u32[]{:S(2)}, u32[]{:S(2)}) async-start(bf16[128,16,1024]{2,1,0:T(8,128)(2,1)} %all-gather.3.cloned.1.call-done), calls=%async_computation | async-start | bytes 8388608 | tf_op jit(solution)/shard_map/all_to_all | solution.py:43
  85.1 142.5 %all-gather.5.cloned.1.call-start = ((), (), s32[]{:S(2)}) async-start(), calls=%async_computation.3 | async-start | bytes 5242880 | tf_op jit(solution)/shard_map/all_gather | solution.py:59
  244.5 11.9 %copy-start.5 = (s32[56]{0:T(128)S(1)}, s32[56]{0:T(128)}, u32[]{:S(2)}) copy-start(s32[56]{0:T(128)} %param.11) | copy-start | bytes 676
  246.5 37.8 %all-to-all-start.1 = ((bf16[2,1024,256]{2,0,1:T(2,128)(2,1)}), bf16[2,1024,256]{2,0,1:T(2,128)(2,1)S(1)}, u32[]{:S(2)}, u32[]{:S(2)}) async-start(bf16[2,1024,256]{2,0,1:T(2,128)(2,1)} %copy.29), calls=%async_computation.1 | async-start | bytes 2097152 | tf_op jit(solution)/shard_map/all_to_all | solution.py:72
  256.4 6.1 %copy-start.1 = (bf16[64,2,16,1024]{3,2,0,1:T(8,128)(2,1)S(1)}, bf16[64,2,16,1024]{3,2,0,1:T(8,128)(2,1)}, u32[]{:S(2)}) copy-start(bf16[64,2,16,1024]{3,2,0,1:T(8,128)(2,1)} %copy.27) | copy-start | bytes 12582916
  256.4 6.1 %copy-start.2 = (f32[2,256,1024]{2,1,0:T(8,128)S(1)}, f32[2,256,1024]{2,1,0:T(8,128)}, u32[]{:S(2)}) copy-start(f32[2,256,1024]{2,1,0:T(8,128)} %param.14) | copy-start | bytes 6291460
Sparse Core Ops, SparseCore 0:
  15.8 57.4 all-gather.2
  87.7 51.7 all-gather.4
where the time goes:
time: 293 us
  blocking collectives  144 us (49%)
  waiting for transfers between devices  77.4 us (26%)
  starting transfers between devices  21.6 us (7%)
  matrix products  16 us (5%)
  between operations  14.3 us (5%)
  other arithmetic  11.1 us (4%)
  local copies, waits for them, and re-layouts  8.6 us (3%)
    psum x1, blocking collectives, local(): adam_sq = lax.psum(jnp.sum(adam * adam, axis=(1, 2)), ('fsdp', 'group'))  136 us
    all_gather x1, waiting for transfers between devices, local(): wide = lax.all_gather(in_slots, 'group', axis=2, tiled=True)  57.6 us
    all_to_all x1, waiting for transfers between devices, local(): lax.all_to_all(direction, 'fsdp', split_axis=1, concat_axis=0, tiled=True)  19.1 us
    all_to_all x1, starting transfers between devices, local(): full = lax.all_to_all(wide, 'fsdp', split_axis=0, concat_axis=1, tiled=True)  11.7 us
    all_to_all x1, starting transfers between devices, local(): lax.all_to_all(direction, 'fsdp', split_axis=1, concat_axis=0, tiled=True)  9.82 us
    psum x1, blocking collectives, local(): precond_sq = lax.psum(jnp.sum(precond * precond, axis=(1, 2)), 'group')  7.73 us
    dot_general x1, matrix products, local(): jnp.einsum('ski,skj->sij', lax.all_gather(left_root, 'group', axis=1, til...  7.13 us
    dot_general x1, matrix products, local(): jnp.einsum('ski,skj->sij', col_block, full, preferred_element_type=jnp.fl...  6.1 us
  transfers between devices with their start and end apart: 4, of which 2 were waited for; matrix products, arithmetic and copies ran while one was open for 5% of the time, Pallas kernels for 0%

commit v1 on v0

v1 whole, which is shorter than its diff:
```python
import jax
import jax.numpy as jnp
from jax import lax
from jax.experimental import pallas as pl
from jax.experimental.pallas import tpu as pltpu
from jax.sharding import PartitionSpec as P

MESH = pl.DeviceIdType.MESH
Z, Y, X = 8, 4, 4
QUADS = Z * Y
EDGE = 1024
NBLK = 56
HALF = EDGE // 2
ROWS, COLS = 16, 256


def drain(ref, sem):
    pltpu.make_async_copy(ref, ref, sem).wait()


def exchange(
    slot_ref,
    rows_ref,
    cols_ref,
    grads_ref,
    second_ref,
    lstat_ref,
    rstat_ref,
    lroot_ref,
    rroot_ref,
    returned,
    moment_ref,
    new_left_ref,
    new_right_ref,
    moments,
    new_left,
    new_right,
    grads,
    second,
    table,
    table_smem,
    pieces,
    gleft_in,
    gright_in,
    block,
    lroot,
    rroot,
    mixed,
    precond,
    direction,
    gleft,
    gright,
    relay,
    cross,
    half_way,
    by_x,
    by_z,
    adam_in,
    adam_sum,
    norm,
    block_send,
    block_recv,
    swap_send,
    swap_recv,
    root_send,
    root_recv,
    row_recv,
    pass_send,
    pass_recv,
    gram_send,
    gram_recv,
    relay_send,
    relay_recv,
    adam_send,
    adam_recv,
    norm_send,
    norm_recv,
    out_send,
    out_recv,
    bulk_send,
    pass_out_send,
    half_way_recv,
    by_x_recv,
    by_z_recv,
    load_sem,
    store_sem,
    table_sem,
):
    f = lax.axis_index("fsdp")
    g = lax.axis_index("group")
    core = lax.rem(f, 2)
    quad = lax.div(f, 2)
    y = lax.rem(quad, Y)
    z = lax.div(quad, Y)
    slot = quad * X + g
    other = f + 1 - 2 * core
    side = lax.div(g, 2)
    parity = lax.rem(g, 2)
    at_home = side == core

    def device(zz, yy, cc):
        return (zz * Y + yy) * 2 + cc

    def remote(src, dst, send, recv, ff, gg):
        pltpu.make_async_remote_copy(
            src_ref=src,
            dst_ref=dst,
            send_sem=send,
            recv_sem=recv,
            device_id=(ff, gg),
            device_id_type=MESH,
        ).start()

    def span(j):
        return pl.ds(pl.multiple_of(lax.rem(j, X) * COLS, COLS), COLS)

    def left_block(ref, j, k):
        return ref.at[span(j), span(k)]

    def send_root(k, ff, xx, lefts, rights):
        for d in lefts:
            src = lroot_ref.at[k, :, span(g + d)]
            remote(src, left_block(lroot, g, g + d), root_send.at[k], root_recv, ff, xx)
        for d in rights:
            src = rroot_ref.at[k, span(g + d), :]
            remote(src, left_block(rroot, g + d, g), root_send.at[k], root_recv, ff, xx)

    for k in range(2):
        home = 2 * core + k
        around = lax.rem(g - home + X, X)

        @pl.when(around == 0)
        def _():
            for src, dst in ((lroot_ref.at[k], lroot.at[span(g)]), (rroot_ref.at[k], rroot.at[:, span(g)])):
                remote(src, dst, root_send.at[k], row_recv, other, g)
                pltpu.make_async_copy(src, dst, row_recv).start()

        @pl.when(around == 1)
        def _():
            send_root(k, quad * 2, home, (0, 1, 2), (0, 1))

        @pl.when(around == 2)
        def _():
            send_root(k, quad * 2, home, (0,), ())
            send_root(k, quad * 2 + 1, home, (), (0,))

        @pl.when(around == 3)
        def _():
            send_root(k, quad * 2 + 1, home, (0, 3), (0, 3, 2))

    load_grads = pltpu.make_async_copy(grads_ref, grads.at[pl.ds(0, NBLK)], load_sem.at[0])
    load_second = pltpu.make_async_copy(second_ref, second, load_sem.at[1])
    load_left = pltpu.make_async_copy(lstat_ref, new_left, load_sem.at[2])
    load_right = pltpu.make_async_copy(rstat_ref, new_right, load_sem.at[3])
    load_grads.start()
    load_second.start()
    lane = lax.broadcasted_iota(jnp.int32, (8, 128), 1)

    def valid(b):
        return (f * ROWS < rows_ref[b]) & (g * COLS < cols_ref[b])

    source = jnp.full((8, 128), NBLK, jnp.int32)
    for b in range(NBLK):
        source = jnp.where(lane == slot_ref[b], jnp.where(valid(b), b, NBLK), source)
    table[...] = source
    to_smem = pltpu.make_async_copy(table, table_smem, table_sem)
    to_smem.start()
    grads[NBLK] = jnp.zeros((ROWS, COLS), jnp.bfloat16)
    to_smem.wait()
    load_grads.wait()

    mine = block.at[quad, core, :, pl.ds(pl.multiple_of(g * COLS, COLS), COLS)]

    def fill(at):
        pieces[at] = grads[table_smem[0, at]]

    across = lax.rem(z + Z // 2, Z) * Y * X
    for way, ff in ((0, device(lax.rem(z + 2, Z), y, core)), (1, device(lax.rem(z + 6, Z), y, core))):
        for n in range(8):
            fill(across + way * 8 + n)
        bulk = pieces.at[pl.ds(across + way * 8, 8)]
        remote(bulk, half_way.at[way], bulk_send, half_way_recv.at[way], ff, g)

    def send_blocks(step, carry):
        dy, dx = lax.div(step, X), lax.rem(step, X)
        yy, xx = lax.rem(y + dy, Y), lax.rem(g + dx, X)
        for dz in (3, 5, 2, 6, 1, 7, 0):
            zz = lax.rem(z + dz, Z)
            at = (zz * Y + yy) * X + xx
            fill(at)
            src = pieces.at[at]
            if dz:
                remote(src, mine, block_send, block_recv, device(zz, yy, core), xx)
            else:

                @pl.when(step == 0)
                def _():
                    pltpu.make_async_copy(src, mine, block_recv).start()

                @pl.when(step != 0)
                def _():
                    remote(src, mine, block_send, block_recv, device(zz, yy, core), xx)

        return carry

    lax.fori_loop(0, X * Y, send_blocks, 0)

    for way in range(2):
        zz, zs = lax.rem(z + (2, 6)[way], Z), lax.rem(z + (6, 2)[way], Z)
        drain(half_way.at[way], half_way_recv.at[way])

        @pl.loop(0, 8)
        def _(n):
            dst = block.at[zs * Y + y, core, :, pl.ds(pl.multiple_of(g * COLS, COLS), COLS)]
            ff = device(zz, 2 * way + lax.div(n, X), core)
            remote(half_way.at[way, n], dst, block_send, block_recv, ff, lax.rem(n, X))

    def pass_on(ref, j, k):
        here = left_block(ref, j, k)
        remote(here, here, pass_send, pass_recv, other, g)

    load_left.start()
    load_right.start()

    load_second.wait()

    def one_block(b, sums):
        grad = jnp.where(valid(b), grads[b].astype(jnp.float32), 0.0)
        moment = 0.95 * second[b] + 0.05 * grad * grad
        moments[b] = moment
        adam = grad / (jnp.sqrt(moment) + 1e-08)
        adam = adam * adam
        adam = adam[0:8] + adam[8:16]
        adam = jnp.sum(adam[:, 0:128] + adam[:, 128:256], keepdims=True)
        return sums + jnp.where(lane == slot_ref[b], adam, 0.0)

    adam_sum[0] = lax.fori_loop(0, NBLK, one_block, jnp.zeros((8, 128), jnp.float32), unroll=4)

    store_moment = pltpu.make_async_copy(moments, moment_ref, store_sem.at[0])
    store_moment.start()

    def adam_stage(stage, first, peers):
        for d, (ff, gg) in enumerate(peers):
            remote(adam_sum.at[stage], adam_in.at[first + d], adam_send.at[stage], adam_recv.at[stage], ff, gg)

    def adam_add(stage, first, count):
        drain(adam_in.at[pl.ds(first, count)], adam_recv.at[stage])
        total = adam_sum[stage]
        for d in range(count):
            total = total + adam_in[first + d]
        return total

    adam_stage(0, 0, [(other, g)])

    drain(lroot.at[pl.ds(0, 6 * COLS // X)], root_recv)

    @pl.when(core == 0)
    def _():
        for ref, j, k in ((lroot, 1, 1), (lroot, 1, 2), (lroot, 1, 3), (lroot, 2, 2), (rroot, 1, 1), (rroot, 2, 1)):
            pass_on(ref, g + j, g + k)

    @pl.when(core == 1)
    def _():
        for ref, j, k in ((lroot, 3, 3), (lroot, 3, 2), (rroot, 3, 3), (rroot, 2, 3), (rroot, 1, 3), (rroot, 2, 2)):
            pass_on(ref, g + j, g + k)

    adam_sum[1] = adam_add(0, 0, 1)
    adam_stage(1, 1, [(f, lax.rem(g + d, X)) for d in range(1, X)])

    drain(lroot.at[pl.ds(0, 2 * COLS)], row_recv)
    drain(lroot.at[pl.ds(0, 6 * COLS // X)], pass_recv)
    for j, k in ((1, 0), (2, 0), (3, 0), (2, 1), (2, 3), (1, 3)):
        rroot[span(g + k), span(g + j)] = rroot[span(g + j), span(g + k)].T
    for j, k in ((0, 1), (0, 2), (0, 3), (1, 2), (3, 2), (1, 3)):
        lroot[span(g + k), span(g + j)] = lroot[span(g + j), span(g + k)].T
    half = pl.ds(pl.multiple_of(core * HALF, HALF), HALF)

    drain(block.at[:, core], block_recv)
    remote(block.at[:, core], block.at[:, core], swap_send, swap_recv, other, g)

    def mix(cc):
        @pl.loop(0, 2)
        def _(m):
            at = pl.ds(pl.multiple_of(m * 16, 16), 16)
            part = block[at, cc].reshape(COLS, EDGE)
            value = jnp.dot(part, rroot[:, half], preferred_element_type=jnp.float32)
            mixed[at, cc] = value.astype(jnp.bfloat16).reshape(16, ROWS, HALF)

    mix(core)
    drain(block.at[:, 1 - core], swap_recv)

    def send_gram(which, m, src, dst):
        xx = 2 * core + m
        ff = quad * 2 + side
        around = lax.rem(xx - g + X, X)
        send = gram_send.at[which, m]

        @pl.when(around == 0)
        def _():
            pltpu.make_async_copy(src.at[m], dst.at[parity], gram_recv.at[which, parity]).start()

        @pl.when(lax.rem(around, 2) == 1)
        def _():
            remote(src.at[m], dst.at[parity], send, gram_recv.at[which, parity], ff, xx)

        @pl.when(around == 2)
        def _():
            for d, gg in ((0, lax.rem(g + 1, X)), (2, lax.rem(g + 3, X))):
                remote(src.at[m, :, span(g + d)], relay.at[which], send, relay_recv.at[which], ff, gg)

    def whole():
        return block[...].reshape(EDGE, EDGE)

    for m in range(2):
        part = block[pl.ds(core * 16 + m * 8, 8)].reshape(COLS, EDGE)
        gleft[m] = lax.dot_general(
            part, whole(), (((1,), (1,)), ((), ())), preferred_element_type=jnp.float32
        ).astype(jnp.bfloat16)
        send_gram(0, m, gleft, gleft_in)

    mix(1 - core)
    adam_sum[2] = adam_add(1, 1, X - 1)
    adam_stage(2, 4, [(device(z, lax.rem(y + d, Y), core), g) for d in range(1, Y)])

    rows_valid, cols_valid = 0, 0
    for b in range(NBLK):
        rows_valid = jnp.where(slot_ref[b] == slot, rows_ref[b], rows_valid)
        cols_valid = jnp.where(slot_ref[b] == slot, cols_ref[b], cols_valid)
    cols_keep = (core * HALF + lax.broadcasted_iota(jnp.int32, (COLS, HALF), 1)) < cols_valid

    def one_part(m, total):
        at = pl.multiple_of(m * COLS, COLS)
        value = jnp.dot(lroot[pl.ds(at, COLS)], mixed[...].reshape(EDGE, HALF), preferred_element_type=jnp.float32)
        rows_keep = (at + lax.broadcasted_iota(jnp.int32, (COLS, HALF), 0)) < rows_valid
        value = jnp.where(rows_keep & cols_keep, value, 0.0)
        precond[pl.ds(at, COLS)] = value
        square = value * value
        return total + jnp.sum(square.reshape(COLS // 8, 8, HALF), axis=0)

    total = lax.fori_loop(0, 4, one_part, jnp.zeros((8, HALF), jnp.float32))
    norm[0] = jnp.broadcast_to(jnp.sum(total, keepdims=True), (8, 128))
    remote(norm.at[0], norm.at[1], norm_send, norm_recv, other, g)

    adam_sum[3] = adam_add(2, 4, Y - 1)
    adam_stage(3, 7, [(device(lax.rem(z + d, Z), y, core), g) for d in range(1, Z)])

    for m in range(2):
        at = pl.multiple_of(core * HALF + m * COLS, COLS)
        part = block[:, :, :, pl.ds(at, COLS)].reshape(EDGE, COLS)
        gright[m] = lax.dot_general(
            part, whole(), (((0,), (0,)), ((), ())), preferred_element_type=jnp.float32
        ).astype(jnp.bfloat16)
        send_gram(1, m, gright, gright_in)

    adam = adam_add(3, 7, Z - 1)
    adam = jnp.sum(jnp.where(lane == slot, adam, 0.0)[0:1], keepdims=True)

    drain(norm.at[1], norm_recv)
    squares = (norm[0] + norm[1])[0:1, 0:1]
    factor = jnp.sqrt(adam) / (jnp.sqrt(squares) + 1e-06)

    @pl.loop(0, 4)
    def _(m):
        at = pl.multiple_of(m * COLS, COLS)
        value = (precond[pl.ds(at, COLS)] * factor).astype(jnp.bfloat16)
        direction[pl.ds(m * 16, 16)] = value.reshape(16, ROWS, HALF)

    def columns(e):
        return pl.ds(pl.multiple_of(e * COLS, COLS), COLS)

    def tie(e):
        return lax.rem(2 * core + e - g + X, X) == 2

    for e in range(2):

        @pl.when(tie(e))
        def _():
            for n, gg in ((0, lax.rem(g + 1, X)), (1, lax.rem(g + 3, X))):
                src = direction.at[pl.ds(n * QUADS, QUADS), :, columns(e)]
                remote(src, by_x, bulk_send, by_x_recv, f, gg)

    for e in range(2):

        @pl.when(jnp.logical_not(tie(e)))
        def _():
            for way, dz in ((0, 2), (1, 6)):
                src = direction.at[pl.ds(lax.rem(z + 4, Z) * 8 + way * 4, 4), :, columns(e)]
                ff = device(lax.rem(z + dz, Z), y, core)
                remote(src, by_z.at[way, e], bulk_send, by_z_recv.at[way, e], ff, g)

    def send_out(step, carry):
        dy, dc = lax.div(step, 2), lax.rem(step, 2)
        yy, cc = lax.rem(y + dy, Y), lax.rem(core + dc, 2)
        for e in range(2):
            xx = 2 * core + e

            @pl.when(jnp.logical_not(tie(e)))
            def _():
                for dz in (3, 5, 2, 6, 1, 7, 0):
                    ff = device(lax.rem(z + dz, Z), yy, cc)
                    src = direction.at[ff, :, columns(e)]
                    dst = returned.at[slot]
                    if dz:
                        remote(src, dst, out_send, out_recv, ff, xx)
                    else:
                        local = (step == 0) & (xx == g)

                        @pl.when(local)
                        def _():
                            pltpu.make_async_copy(src, dst, out_recv).start()

                        @pl.when(jnp.logical_not(local))
                        def _():
                            remote(src, dst, out_send, out_recv, ff, xx)

        return carry

    lax.fori_loop(0, 8, send_out, 0)

    drain(by_x, by_x_recv)
    left_neighbour = lax.rem(g + 3, X)
    from_left = lax.div(left_neighbour, 2) != core
    origin = jnp.where(from_left, left_neighbour, lax.rem(g + 1, X))
    first = jnp.where(from_left, 0, QUADS)

    def on_x(n, carry):
        at = lax.rem(n + quad, QUADS)
        remote(by_x.at[at], returned.at[quad * X + origin], pass_out_send, out_recv, first + at, lax.rem(origin + 2, X))
        return carry

    lax.fori_loop(0, QUADS, on_x, 0)

    for e in range(2):

        @pl.when(jnp.logical_not(tie(e)))
        def _():
            for way in range(2):
                zz, zs = lax.rem(z + (2, 6)[way], Z), lax.rem(z + (6, 2)[way], Z)
                drain(by_z.at[way, e], by_z_recv.at[way, e])

                @pl.loop(0, 4)
                def _(n):
                    dst = returned.at[(zs * Y + y) * X + g]
                    remote(by_z.at[way, e, n], dst, pass_out_send, out_recv, zz * 8 + way * 4 + n, 2 * core + e)

    arounds = [lax.rem(g - 2 * core - k + X, X) for k in range(2)]
    for which, gram in ((0, gleft_in), (1, gright_in)):
        for k in range(2):
            for way in (1, 3):

                @pl.when(arounds[k] == way)
                def _():
                    drain(gram.at[k], gram_recv.at[which, k])
                    drain(relay.at[which], relay_recv.at[which])
                    gg = lax.rem(g + way, X)
                    here = gram.at[k, :, span(g + way)]
                    send = relay_send.at[which]
                    recv = gram_recv.at[which, k]
                    remote(here, cross.at[which, way // 2], send, recv, f, gg)
                    column = span(g + 3)
                    remote(relay.at[which], gram.at[k, :, column], send, recv, f, gg)

    def update(target, gram, k):
        @pl.loop(0, 8)
        def _(m):
            at = pl.ds(pl.multiple_of(m * 32, 32), 32)
            target[k, at] = 0.9 * target[k, at] + 0.1 * gram[k, at].astype(jnp.float32)

    store_left = [pltpu.make_async_copy(new_left.at[k], new_left_ref.at[k], store_sem.at[1 + k]) for k in range(2)]
    store_right = [pltpu.make_async_copy(new_right.at[k], new_right_ref.at[k], store_sem.at[3 + k]) for k in range(2)]
    parts = ((0, new_left, gleft_in, store_left), (1, new_right, gright_in, store_right))
    load_left.wait()
    load_right.wait()
    for last in (False, True):
        for which, target, gram, store in parts:
            for k in range(2):

                @pl.when((arounds[k] == 2) == last)
                def _():
                    if last:
                        drain(gram.at[k], gram_recv.at[which, k])
                        gram[k, :, span(g + 3)] = cross[which, 0].T
                        gram[k, :, span(g + 1)] = cross[which, 1].T
                    else:

                        @pl.when(arounds[k] == 0)
                        def _():
                            drain(gram.at[k], gram_recv.at[which, k])

                    update(target, gram, k)
                    store[k].start()

    drain(pieces.at[pl.ds(0, QUADS * X - 1)], block_send)
    drain(block.at[:, core], swap_send)
    drain(lroot.at[pl.ds(0, 6 * COLS // X)], pass_send)
    drain(norm.at[0], norm_send)
    drain(adam_in.at[0], adam_send.at[0])
    drain(adam_in.at[pl.ds(0, 3)], adam_send.at[1])
    drain(adam_in.at[pl.ds(0, 3)], adam_send.at[2])
    drain(adam_in.at[pl.ds(0, 7)], adam_send.at[3])
    for k in range(2):
        around = lax.rem(g - 2 * core - k + X, X)
        for steps, blocks in ((0, 8), (1, 5), (2, 2), (3, 5)):

            @pl.when(around == steps)
            def _():
                drain(lroot.at[pl.ds(0, blocks * COLS // X)], root_send.at[k])

        around = lax.rem(2 * core + k - g + X, X)
        for which in range(2):

            @pl.when(lax.rem(around, 2) == 1)
            def _():
                drain(gleft.at[k], gram_send.at[which, k])

            @pl.when(around == 2)
            def _():
                drain(relay, gram_send.at[which, k])

    for which in range(2):
        drain(relay, relay_send.at[which])

    @pl.when(at_home)
    def _():
        drain(pieces.at[pl.ds(0, 2 * 56 - 1)], out_send)
        drain(pieces.at[pl.ds(0, 32 + 16)], pass_out_send)
        drain(pieces.at[pl.ds(0, 16 + 16)], bulk_send)

    @pl.when(jnp.logical_not(at_home))
    def _():
        drain(pieces.at[pl.ds(0, 56)], out_send)
        drain(pieces.at[pl.ds(0, 32 + 8)], pass_out_send)
        drain(pieces.at[pl.ds(0, 16 + 64 + 8)], bulk_send)

    drain(returned, out_recv)

    store_moment.wait()
    for store in store_left + store_right:
        store.wait()


def hand_over(
    slot_ref,
    returned,
    moment_in,
    left_in,
    right_in,
    directions,
    moment,
    left,
    right,
    left_held,
    right_held,
    moment_held,
    held,
    in_sem,
    out_sem,
    piece_sem,
):
    @pl.loop(0, NBLK)
    def _(b):
        pltpu.make_async_copy(returned.at[slot_ref[b]], held.at[b], piece_sem.at[0]).start()

    steps = []
    for src, kept, dst, count in (
        (left_in, left_held, left, 4),
        (right_in, right_held, right, 4),
        (moment_in, moment_held, moment, 2),
    ):
        size = dst.shape[0] // count
        for n in range(count):
            at = pl.ds(n * size, size)
            load = pltpu.make_async_copy(src.at[at], kept.at[at], in_sem.at[len(steps)])
            store = pltpu.make_async_copy(kept.at[at], dst.at[at], out_sem.at[len(steps)])
            load.start()
            steps.append((load, store))
    drain(held, piece_sem.at[0])
    last = pltpu.make_async_copy(held, directions, piece_sem.at[1])
    last.start()
    for load, store in steps:
        load.wait()
        store.start()
    for _, store in steps:
        store.wait()
    last.wait()


def run_exchange(grads, second_moment, slot_of, block_rows, block_cols, *matrices):
    half = jnp.bfloat16
    away = pl.BlockSpec(memory_space=pl.ANY)
    numbers = pl.BlockSpec(memory_space=pltpu.SMEM)
    dma = pltpu.SemaphoreType.DMA
    returned, moment, left, right = pl.pallas_call(
        exchange,
        out_shape=(
            jax.ShapeDtypeStruct((QUADS * X, ROWS, COLS), half),
            jax.ShapeDtypeStruct((NBLK, ROWS, COLS), jnp.float32),
            jax.ShapeDtypeStruct((2, COLS, EDGE), jnp.float32),
            jax.ShapeDtypeStruct((2, COLS, EDGE), jnp.float32),
        ),
        in_specs=[numbers] * 3 + [away] * 6,
        out_specs=(away, away, away, away),
        scratch_shapes=[
            pltpu.VMEM((NBLK, ROWS, COLS), jnp.float32),
            pltpu.VMEM((2, COLS, EDGE), jnp.float32),
            pltpu.VMEM((2, COLS, EDGE), jnp.float32),
            pltpu.VMEM((NBLK + 1, ROWS, COLS), half),
            pltpu.VMEM((NBLK, ROWS, COLS), jnp.float32),
            pltpu.VMEM((8, 128), jnp.int32),
            pltpu.SMEM((8, 128), jnp.int32),
            pltpu.VMEM((QUADS * X, ROWS, COLS), half),
            pltpu.VMEM((2, COLS, EDGE), half),
            pltpu.VMEM((2, COLS, EDGE), half),
            pltpu.VMEM((QUADS, 2, ROWS, EDGE), half),
            pltpu.VMEM((EDGE, EDGE), half),
            pltpu.VMEM((EDGE, EDGE), half),
            pltpu.VMEM((QUADS, 2, ROWS, HALF), half),
            pltpu.VMEM((EDGE, HALF), jnp.float32),
            pltpu.VMEM((QUADS * 2, ROWS, HALF), half),
            pltpu.VMEM((2, COLS, EDGE), half),
            pltpu.VMEM((2, COLS, EDGE), half),
            pltpu.VMEM((2, COLS, COLS), half),
            pltpu.VMEM((2, 2, COLS, COLS), half),
            pltpu.VMEM((2, 8, ROWS, COLS), half),
            pltpu.VMEM((QUADS, ROWS, COLS), half),
            pltpu.VMEM((2, 2, 4, ROWS, COLS), half),
            pltpu.VMEM((14, 8, 128), jnp.float32),
            pltpu.VMEM((4, 8, 128), jnp.float32),
            pltpu.VMEM((2, 8, 128), jnp.float32),
            dma,
            dma,
            dma,
            dma,
            dma((2,)),
            dma,
            dma,
            dma,
            dma,
            dma((2, 2)),
            dma((2, 2)),
            dma((2,)),
            dma((2,)),
            dma((4,)),
            dma((4,)),
            dma,
            dma,
            dma,
            dma,
            dma,
            dma,
            dma((2,)),
            dma,
            dma((2, 2)),
            dma((4,)),
            dma((5,)),
            dma,
        ],
        compiler_params=pltpu.CompilerParams(
            has_side_effects=True, vmem_limit_bytes=56 * 1024 * 1024
        ),
        cost_estimate=pl.CostEstimate(
            flops=8 * EDGE * EDGE * HALF, bytes_accessed=8 * EDGE * EDGE, transcendentals=0
        ),
    )(slot_of, block_rows, block_cols, grads, second_moment, *matrices)
    rows = (2 * COLS, EDGE)
    directions, moment, left, right = pl.pallas_call(
        hand_over,
        out_shape=(
            jax.ShapeDtypeStruct(grads.shape, half),
            jax.ShapeDtypeStruct(moment.shape, moment.dtype),
            jax.ShapeDtypeStruct(rows, left.dtype),
            jax.ShapeDtypeStruct(rows, right.dtype),
        ),
        in_specs=[numbers] + [away] * 4,
        out_specs=(away, away, away, away),
        scratch_shapes=[
            pltpu.VMEM(rows, left.dtype),
            pltpu.VMEM(rows, right.dtype),
            pltpu.VMEM(moment.shape, moment.dtype),
            pltpu.VMEM(grads.shape, half),
            dma((10,)),
            dma((10,)),
            dma((2,)),
        ],
        compiler_params=pltpu.CompilerParams(vmem_limit_bytes=56 * 1024 * 1024),
    )(slot_of, returned, moment, left.reshape(rows), right.reshape(rows))
    shape = matrices[0].shape
    return directions, moment, left.reshape(shape), right.reshape(shape)


def solution(mesh):
    placed = (
        P(None, "fsdp", "group"),
        P(None, "fsdp", "group"),
        P(),
        P(),
        P(),
        P("fsdp", "group", None),
        P("fsdp", "group", None),
        P("fsdp", "group", None),
        P("fsdp", None, "group"),
    )
    return jax.shard_map(
        run_exchange,
        mesh=mesh,
        in_specs=placed,
        out_specs=(
            P(None, "fsdp", "group"),
            P(None, "fsdp", "group"),
            P("fsdp", "group", None),
            P("fsdp", "group", None),
        ),
        check_vma=False,
    )
```

time: 293 us -> 97.5 us (0.33)
  blocking collectives: 144 us -> 0 us
  Pallas kernels: 0 us -> 95 us
  waiting for transfers between devices: 77.4 us -> 0 us
  starting transfers between devices: 21.6 us -> 0 us
  matrix products: 16 us -> 0 us
  between operations: 14.3 us -> 0.64 us
  other arithmetic: 11.1 us -> 0 us
  local copies, waits for them, and re-layouts: 8.6 us -> 0 us
    psum x2 -> x0, blocking collectives: 144 us -> none  [the longest x1 136 us: local(): adam_sq = lax.psum(jnp.sum(adam * adam, axis=(1, 2)), ('fsdp', 'group'))]
    pallas_call x0 -> x2, Pallas kernels: none -> 95 us  [the longest x1 89 us: run_exchange(): pl.pallas_call(exchange, out_shape=(jax.ShapeDtypeStruct((QUADS * X, ROWS...]
    all_gather x2 -> x0, waiting for transfers between devices: 57.6 us -> none  [the longest x1 57.6 us: local(): wide = lax.all_gather(in_slots, 'group', axis=2, tiled=True)]
    all_to_all x2 -> x0, starting transfers between devices: 21.6 us -> none  [the longest x1 11.7 us: local(): full = lax.all_to_all(wide, 'fsdp', split_axis=0, concat_axis=1, tiled=True)]
    all_to_all x2 -> x0, waiting for transfers between devices: 19.1 us -> none  [the longest x1 19.1 us: local(): lax.all_to_all(direction, 'fsdp', split_axis=1, concat_axis=0, tiled=True)]
    dot_general x3 -> x0, matrix products: 16 us -> none  [the longest x1 7.13 us: local(): jnp.einsum('ski,skj->sij', lax.all_gather(left_root, 'group', axis=1, til...]
    all_to_all x3 -> x0, local copies, waits for them, and re-layouts: 5.28 us -> none  [the longest x1 5 us: local(): full = lax.all_to_all(wide, 'fsdp', split_axis=0, concat_axis=1, tiled=True)]
    reduce_sum x4 -> x0, other arithmetic: 4.17 us -> none  [the longest x1 3.13 us: local(): adam_sq = lax.psum(jnp.sum(adam * adam, axis=(1, 2)), ('fsdp', 'group'))]
  transfers between devices with their start and end apart: 4 -> 0, of which waited for: 2 -> 0; matrix products, arithmetic and copies ran while one was open for 5% -> 0% of each run, Pallas kernels for 0% -> 0%
where the time goes in v1:
time: 97.5 us; the launch traced here: 95.7 us
  Pallas kernels  95 us (97%)
    pallas_call x1, Pallas kernels, run_exchange(): pl.pallas_call(exchange, out_shape=(jax.ShapeDtypeStruct((QUADS * X, ROWS...  89 us
    pallas_call x1, Pallas kernels, run_exchange(): pl.pallas_call(hand_over, out_shape=(jax.ShapeDtypeStruct(grads.shape, ha...  6.01 us

profile of v1, /device:TPU:1, one launch (start us, length us, event | category | flops | bytes accessed | tf_op | source)
XLA Modules:
  0.0 95.7 jit_solution(13506712062321867414)
XLA Ops:
  0.6 89.0 %shard_map.120 = (bf16[128,16,256]{2,1,0:T(8,128)(2,1)}, f32[56,16,256]{2,1,0:T(8,128)}, f32[2,256,1024]{2,1,0:T(8,128)}, f32[2,256,1024]{2,1,0:T(8,128)}) custom-call(s32[56]{0:T(128)} %slot_ref.3, s32[56]{0:T(128)} %rows_ref.1, s32[56]{0:T(128)} %cols_ref.1, bf16[56,16,256]{2,1,0:T(8,128)(2,1)} %grads_ref.1, f32[56,16,256]{2,1,0:T(8,128)} %second_ref.1, ...), custom_call_target="tpu_custom_call" | custom-call | flops 4294967296 | bytes 8388608 | tf_op jit(solution)/shard_map/pallas_call | solution.py:593
  89.6 6.0 %shard_map.121 = (bf16[56,16,256]{2,1,0:T(8,128)(2,1)}, f32[56,16,256]{2,1,0:T(8,128)}, f32[512,1024]{1,0:T(8,128)}, f32[512,1024]{1,0:T(8,128)}) custom-call(s32[56]{0:T(128)} %slot_ref.3, bf16[128,16,256]{2,1,0:T(8,128)(2,1)} %get-tuple-element.12.returned, f32[56,16,256]{2,1,0:T(8,128)} %get-tuple-element.13.moment_in, f32[512,1024]{1,0:T(8,128)} %bitcast.4, ...), custom_call_target="tpu_custom_call" | custom-call | tf_op jit(solution)/shard_map/pallas_call | solution.py:666

commit v2 on v1

v2 whole, which is shorter than its diff:
```python
import jax
import jax.numpy as jnp
from jax import lax
from jax.experimental import pallas as pl
from jax.experimental.pallas import tpu as pltpu
from jax.sharding import PartitionSpec as P

MESH = pl.DeviceIdType.MESH
Z, Y, X = 8, 4, 4
QUADS = Z * Y
EDGE = 1024
NBLK = 56
HALF = EDGE // 2
ROWS, COLS = 16, 256
FAR_FIRST = (4, 3, 5, 2, 6, 1, 7, 0)


def drain(ref, sem):
    pltpu.make_async_copy(ref, ref, sem).wait()


def exchange(
    slot_ref,
    rows_ref,
    cols_ref,
    grads_ref,
    second_ref,
    lstat_ref,
    rstat_ref,
    lroot_ref,
    rroot_ref,
    directions_ref,
    moment_ref,
    new_left_ref,
    new_right_ref,
    returned,
    directions,
    moments,
    new_left,
    new_right,
    grads,
    second,
    table,
    table_smem,
    matches,
    adam_parts,
    pieces,
    gleft_in,
    gright_in,
    block,
    lroot,
    rroot,
    mixed,
    precond,
    direction,
    gleft,
    gright,
    gram_part,
    relay,
    cross,
    adam_in,
    adam_sum,
    norm,
    block_send,
    block_recv,
    swap_send,
    swap_recv,
    root_send,
    root_recv,
    row_recv,
    pass_send,
    pass_recv,
    gram_send,
    gram_recv,
    relay_send,
    relay_recv,
    adam_send,
    adam_recv,
    norm_send,
    norm_recv,
    out_send,
    out_recv,
    load_sem,
    store_sem,
    table_sem,
):
    f = lax.axis_index("fsdp")
    g = lax.axis_index("group")
    core = lax.rem(f, 2)
    quad = lax.div(f, 2)
    y = lax.rem(quad, Y)
    z = lax.div(quad, Y)
    slot = quad * X + g
    other = f + 1 - 2 * core
    side = lax.div(g, 2)
    parity = lax.rem(g, 2)
    at_home = side == core

    def device(zz, yy, cc):
        return (zz * Y + yy) * 2 + cc

    def remote(src, dst, send, recv, ff, gg):
        pltpu.make_async_remote_copy(
            src_ref=src,
            dst_ref=dst,
            send_sem=send,
            recv_sem=recv,
            device_id=(ff, gg),
            device_id_type=MESH,
        ).start()

    def span(j):
        return pl.ds(pl.multiple_of(lax.rem(j, X) * COLS, COLS), COLS)

    def left_block(ref, j, k):
        return ref.at[span(j), span(k)]

    def send_rows():
        for k in range(2):

            @pl.when(lax.rem(g - 2 * core - k + X, X) == 0)
            def _():
                for src, dst in (
                    (lroot_ref.at[k], lroot.at[span(g)]),
                    (rroot_ref.at[k], rroot.at[:, span(g)]),
                ):
                    remote(src, dst, root_send.at[k], row_recv, other, g)
                    pltpu.make_async_copy(src, dst, row_recv).start()

    PLAN = (
        (1, 0, (((), (0, 1)), ((0, 1), ()), ((2,), ()))),
        (2, 0, (((), ()), ((0,), ()), ((), ()))),
        (2, 1, (((), (0,)), ((), ()), ((), ()))),
        (3, 1, (((), (0, 3)), ((0,), (2,)), ((3,), ()))),
    )

    def send_roots(turn, quarter):
        at = pl.multiple_of(quarter * 64, 64)
        for k in range(2):
            home = 2 * core + k
            for steps, cc, turns in PLAN:
                lefts, rights = turns[turn]
                if lefts or rights:

                    @pl.when(lax.rem(g - home + X, X) == steps)
                    def _():
                        for d in lefts:
                            src = lroot_ref.at[k, pl.ds(at, 64), span(g + d)]
                            dst = lroot.at[pl.ds(pl.multiple_of(g * COLS + at, 64), 64), span(g + d)]
                            remote(src, dst, root_send.at[k], root_recv, quad * 2 + cc, home)
                        for d in rights:
                            row = pl.ds(pl.multiple_of(lax.rem(g + d, X) * COLS + at, 64), 64)
                            src = rroot_ref.at[k, row, :]
                            remote(src, rroot.at[row, span(g)], root_send.at[k], root_recv, quad * 2 + cc, home)

    load_grads = pltpu.make_async_copy(grads_ref, grads.at[pl.ds(0, NBLK)], load_sem.at[0])
    load_second = pltpu.make_async_copy(second_ref, second, load_sem.at[1])
    load_left = pltpu.make_async_copy(lstat_ref, new_left, load_sem.at[2])
    load_right = pltpu.make_async_copy(rstat_ref, new_right, load_sem.at[3])
    load_grads.start()
    load_second.start()
    lane = lax.broadcasted_iota(jnp.int32, (8, 128), 1)

    def valid(b):
        return (f * ROWS < rows_ref[b]) & (g * COLS < cols_ref[b])

    source = jnp.full((8, 128), NBLK, jnp.int32)
    for b in range(NBLK):
        match = lane == slot_ref[b]
        source = jnp.where(match, jnp.where(valid(b), b, NBLK), source)
        matches[pl.ds(b, 1)] = match[0:1].astype(jnp.int32)
    table[...] = source
    to_smem = pltpu.make_async_copy(table, table_smem, table_sem)
    to_smem.start()
    grads[NBLK] = jnp.zeros((ROWS, COLS), jnp.bfloat16)
    to_smem.wait()
    load_grads.wait()

    mine = block.at[z, y, core, :, pl.ds(pl.multiple_of(g * COLS, COLS), COLS)]

    @pl.loop(0, QUADS * X // 8)
    def _(n):
        for k in range(8):
            pieces[n * 8 + k] = grads[table_smem[0, n * 8 + k]]

    def send_blocks(dy):
        yy = lax.rem(y + dy, Y)

        def step(dx, carry):
            xx = lax.rem(g + dx, X)
            for dz in FAR_FIRST:
                zz = lax.rem(z + dz, Z)
                src = pieces.at[(zz * Y + yy) * X + xx]
                to = (src, mine, block_send, block_recv.at[dy], device(zz, yy, core), xx)
                if dy or dz:
                    remote(*to)
                else:

                    @pl.when(dx == 0)
                    def _():
                        pltpu.make_async_copy(src, mine, block_recv.at[dy]).start()

                    @pl.when(dx != 0)
                    def _():
                        remote(*to)

                if dz == 2 and dy < 3:
                    send_roots(dy, dx)
            return carry

        lax.fori_loop(0, X, step, 0)

    def adam_stage(stage, first, peers):
        for d, (ff, gg) in enumerate(peers):
            remote(adam_sum.at[stage], adam_in.at[first + d], adam_send.at[stage], adam_recv.at[stage], ff, gg)

    def adam_add(stage, first, count):
        drain(adam_in.at[pl.ds(first, count)], adam_recv.at[stage])
        total = adam_sum[stage]
        for d in range(count):
            total = total + adam_in[first + d]
        return total

    send_blocks(0)

    load_second.wait()

    def one_block(b, carry):
        grad = jnp.where(valid(b), grads[b].astype(jnp.float32), 0.0)
        moment = 0.95 * second[b] + 0.05 * grad * grad
        moments[b] = moment
        adam = grad / (jnp.sqrt(moment) + 1e-08)
        adam = adam * adam
        adam = adam[0:8] + adam[8:16]
        adam_parts[b] = adam[:, 0:128] + adam[:, 128:256]
        return carry

    lax.fori_loop(0, NBLK, one_block, 0, unroll=4)
    adam = jnp.sum(jnp.sum(adam_parts[...], axis=1), axis=1, keepdims=True)
    adam = jnp.where(matches[...] != 0, adam, 0.0)
    adam_sum[0] = jnp.broadcast_to(jnp.sum(adam, axis=0, keepdims=True), (8, 128))
    store_moment = pltpu.make_async_copy(moments, moment_ref, store_sem.at[0])
    store_moment.start()

    adam_stage(0, 0, [(other, g)])
    send_blocks(1)
    adam_sum[1] = adam_add(0, 0, 1)
    adam_stage(1, 1, [(f, lax.rem(g + d, X)) for d in range(1, X)])
    send_blocks(2)
    send_rows()
    adam_sum[2] = adam_add(1, 1, X - 1)
    adam_stage(2, 4, [(device(z, lax.rem(y + d, Y), core), g) for d in range(1, Y)])
    send_blocks(3)
    load_left.start()
    load_right.start()

    def pass_on(ref, j, k):
        here = left_block(ref, j, k)
        remote(here, here, pass_send, pass_recv, other, g)

    drain(lroot.at[pl.ds(0, 6 * COLS // X)], root_recv)

    @pl.when(core == 0)
    def _():
        for ref, j, k in ((lroot, 1, 1), (lroot, 1, 2), (lroot, 1, 3), (lroot, 2, 2), (rroot, 1, 1), (rroot, 2, 1)):
            pass_on(ref, g + j, g + k)

    @pl.when(core == 1)
    def _():
        for ref, j, k in ((lroot, 3, 3), (lroot, 3, 2), (rroot, 3, 3), (rroot, 2, 3), (rroot, 1, 3), (rroot, 2, 2)):
            pass_on(ref, g + j, g + k)

    adam_sum[3] = adam_add(2, 4, Y - 1)
    adam_stage(3, 7, [(device(lax.rem(z + d, Z), y, core), g) for d in range(1, Z)])

    drain(lroot.at[pl.ds(0, 2 * COLS)], row_recv)
    drain(lroot.at[pl.ds(0, 6 * COLS // X)], pass_recv)
    for j, k in ((1, 0), (2, 0), (3, 0), (2, 1), (2, 3), (1, 3)):
        rroot[span(g + k), span(g + j)] = rroot[span(g + j), span(g + k)].T
    for j, k in ((0, 1), (0, 2), (0, 3), (1, 2), (3, 2), (1, 3)):
        lroot[span(g + k), span(g + j)] = lroot[span(g + j), span(g + k)].T
    half = pl.ds(pl.multiple_of(core * HALF, HALF), HALF)

    def send_gram(which, m, src, dst, at, size):
        xx = 2 * core + m
        ff = quad * 2 + side
        around = lax.rem(xx - g + X, X)
        send = gram_send.at[which, m]
        rows = pl.ds(at if isinstance(at, int) else pl.multiple_of(at, 16), size)

        @pl.when(around == 0)
        def _():
            here, there = src.at[m, rows], dst.at[parity, rows]
            pltpu.make_async_copy(here, there, gram_recv.at[which, parity]).start()

        @pl.when(lax.rem(around, 2) == 1)
        def _():
            here, there = src.at[m, rows], dst.at[parity, rows]
            remote(here, there, send, gram_recv.at[which, parity], ff, xx)

        @pl.when(around == 2)
        def _():
            for d, gg in ((0, lax.rem(g + 1, X)), (2, lax.rem(g + 3, X))):
                here = src.at[m, rows, span(g + d)]
                remote(here, relay.at[which, rows], send, relay_recv.at[which], ff, gg)

    def swap(d):
        ys = lax.rem(y + Y - d, Y)
        rows = block.at[:, ys, core]
        drain(rows, block_recv.at[d])
        remote(rows, rows, swap_send, swap_recv.at[d], other, g)

    def group(d):
        ys = lax.rem(y + Y - d, Y)
        drain(block.at[:, ys, 1 - core], swap_recv.at[d])
        for m in range(2):
            at = pl.multiple_of(core * HALF + m * COLS, COLS)
            value = lax.dot_general(
                block[:, ys, :, :, pl.ds(at, COLS)].reshape(COLS, COLS),
                block[:, ys].reshape(COLS, EDGE),
                (((0,), (0,)), ((), ())),
                preferred_element_type=jnp.float32,
            )
            if d:
                value = gram_part[m] + value
            if d < Y - 1:
                gram_part[m] = value
            else:
                gright[m] = value.astype(jnp.bfloat16)
                send_gram(1, m, gright, gright_in, 0, 128)
        value = jnp.dot(
            block[:, ys].reshape(COLS, EDGE), rroot[:, half], preferred_element_type=jnp.float32
        )
        mixed[:, ys] = value.astype(jnp.bfloat16).reshape(Z, 2, ROWS, HALF)

    swap(0)
    swap(1)
    group(0)
    swap(2)
    group(1)
    swap(3)
    group(2)
    group(3)

    rows_valid, cols_valid = 0, 0
    for b in range(NBLK):
        rows_valid = jnp.where(slot_ref[b] == slot, rows_ref[b], rows_valid)
        cols_valid = jnp.where(slot_ref[b] == slot, cols_ref[b], cols_valid)
    cols_keep = (core * HALF + lax.broadcasted_iota(jnp.int32, (COLS, HALF), 1)) < cols_valid

    def one_part(m, total):
        at = pl.multiple_of(m * COLS, COLS)
        value = jnp.dot(lroot[pl.ds(at, COLS)], mixed[...].reshape(EDGE, HALF), preferred_element_type=jnp.float32)
        rows_keep = (at + lax.broadcasted_iota(jnp.int32, (COLS, HALF), 0)) < rows_valid
        value = jnp.where(rows_keep & cols_keep, value, 0.0)
        precond[pl.ds(at, COLS)] = value
        square = value * value
        return total + jnp.sum(square.reshape(COLS // 8, 8, HALF), axis=0)

    total = lax.fori_loop(0, 4, one_part, jnp.zeros((8, HALF), jnp.float32))
    norm[0] = jnp.broadcast_to(jnp.sum(total, keepdims=True), (8, 128))
    remote(norm.at[0], norm.at[1], norm_send, norm_recv, other, g)

    for m in range(2):
        gleft[m] = lax.dot_general(
            block[pl.ds(core * 4 + m * 2, 2)].reshape(COLS, EDGE),
            block[...].reshape(EDGE, EDGE),
            (((1,), (1,)), ((), ())),
            preferred_element_type=jnp.float32,
        ).astype(jnp.bfloat16)

    adam = adam_add(3, 7, Z - 1)
    adam = jnp.sum(jnp.where(lane == slot, adam, 0.0)[0:1], keepdims=True)

    drain(norm.at[1], norm_recv)
    squares = (norm[0] + norm[1])[0:1, 0:1]
    factor = jnp.sqrt(adam) / (jnp.sqrt(squares) + 1e-06)

    @pl.loop(0, 4)
    def _(m):
        at = pl.multiple_of(m * COLS, COLS)
        value = (precond[pl.ds(at, COLS)] * factor).astype(jnp.bfloat16)
        direction[pl.ds(m * 16, 16)] = value.reshape(16, ROWS, HALF)

    def send_out(step, carry):
        dy, dc, e = lax.div(step, 4), lax.rem(lax.div(step, 2), 2), lax.rem(step, 2)
        yy, cc, xx = lax.rem(y + dy, Y), lax.rem(core + dc, 2), 2 * core + e
        for dz in FAR_FIRST:
            ff = device(lax.rem(z + dz, Z), yy, cc)
            src = direction.at[ff, :, pl.ds(pl.multiple_of(e * COLS, COLS), COLS)]
            dst = returned.at[slot]
            if dz:
                remote(src, dst, out_send, out_recv, ff, xx)
            else:
                local = (step < 2) & at_home & (parity == e)

                @pl.when(local)
                def _():
                    pltpu.make_async_copy(src, dst, out_recv).start()

                @pl.when(jnp.logical_not(local))
                def _():
                    remote(src, dst, out_send, out_recv, ff, xx)

            if dz in (3, 6):
                m = 0 if dz == 3 else 1
                send_gram(0, m, gleft, gleft_in, step * 16, 16)

            if dz in (2, 7):
                m = 0 if dz == 2 else 1

                @pl.when(lax.rem(step, 2) == 0)
                def _():
                    send_gram(1, m, gright, gright_in, 128 + step * 8, 16)

        return carry

    lax.fori_loop(0, 16, send_out, 0)

    arounds = [lax.rem(g - 2 * core - k + X, X) for k in range(2)]
    for which, gram in ((1, gright_in), (0, gleft_in)):
        for k in range(2):
            for way in (1, 3):

                @pl.when(arounds[k] == way)
                def _():
                    drain(gram.at[k], gram_recv.at[which, k])
                    drain(relay.at[which], relay_recv.at[which])
                    gg = lax.rem(g + way, X)
                    here = gram.at[k, :, span(g + way)]
                    send = relay_send.at[which]
                    recv = gram_recv.at[which, k]
                    remote(here, cross.at[which, way // 2], send, recv, f, gg)
                    column = span(g + 3)
                    remote(relay.at[which], gram.at[k, :, column], send, recv, f, gg)

    def update(target, gram, k):
        @pl.loop(0, 8)
        def _(m):
            at = pl.ds(pl.multiple_of(m * 32, 32), 32)
            target[k, at] = 0.9 * target[k, at] + 0.1 * gram[k, at].astype(jnp.float32)

    store_left = [pltpu.make_async_copy(new_left.at[k], new_left_ref.at[k], store_sem.at[1 + k]) for k in range(2)]
    store_right = [pltpu.make_async_copy(new_right.at[k], new_right_ref.at[k], store_sem.at[3 + k]) for k in range(2)]
    parts = ((1, new_right, gright_in, store_right), (0, new_left, gleft_in, store_left))
    load_left.wait()
    load_right.wait()
    for last in (False, True):
        for which, target, gram, store in parts:
            for k in range(2):

                @pl.when((arounds[k] == 2) == last)
                def _():
                    if last:
                        drain(gram.at[k], gram_recv.at[which, k])
                        gram[k, :, span(g + 3)] = cross[which, 0].T
                        gram[k, :, span(g + 1)] = cross[which, 1].T
                    else:

                        @pl.when(arounds[k] == 0)
                        def _():
                            drain(gram.at[k], gram_recv.at[which, k])

                    update(target, gram, k)
                    store[k].start()

    drain(pieces.at[pl.ds(0, QUADS * X - 1)], block_send)
    drain(pieces, swap_send)
    drain(lroot.at[pl.ds(0, 6 * COLS // X)], pass_send)
    drain(norm.at[0], norm_send)
    drain(adam_in.at[0], adam_send.at[0])
    drain(adam_in.at[pl.ds(0, 3)], adam_send.at[1])
    drain(adam_in.at[pl.ds(0, 3)], adam_send.at[2])
    drain(adam_in.at[pl.ds(0, 7)], adam_send.at[3])
    for k in range(2):
        around = lax.rem(g - 2 * core - k + X, X)
        for steps, blocks in ((0, 8), (1, 5), (2, 2), (3, 5)):

            @pl.when(around == steps)
            def _():
                drain(lroot.at[pl.ds(0, blocks * COLS // X)], root_send.at[k])

        around = lax.rem(2 * core + k - g + X, X)
        for which in range(2):

            @pl.when(lax.rem(around, 2) == 1)
            def _():
                drain(gleft.at[k], gram_send.at[which, k])

            @pl.when(around == 2)
            def _():
                drain(relay, gram_send.at[which, k])

    for which in range(2):
        drain(relay, relay_send.at[which])

    @pl.when(at_home)
    def _():
        drain(pieces.at[pl.ds(0, QUADS * X - 1)], out_send)

    @pl.when(jnp.logical_not(at_home))
    def _():
        drain(pieces, out_send)

    drain(returned, out_recv)

    def one_direction(b, carry):
        directions[b] = returned[slot_ref[b]]
        return carry

    lax.fori_loop(0, NBLK, one_direction, 0, unroll=8)
    store_directions = pltpu.make_async_copy(directions, directions_ref, store_sem.at[5])
    store_directions.start()
    store_directions.wait()

    store_moment.wait()
    for store in store_left + store_right:
        store.wait()


def run_exchange(grads, second_moment, slot_of, block_rows, block_cols, *matrices):
    half = jnp.bfloat16
    away = pl.BlockSpec(memory_space=pl.ANY)
    numbers = pl.BlockSpec(memory_space=pltpu.SMEM)
    dma = pltpu.SemaphoreType.DMA
    operands = (slot_of, block_rows, block_cols, grads, second_moment, *matrices)
    return pl.pallas_call(
        exchange,
        out_shape=(
            pltpu.VMEM((NBLK, ROWS, COLS), half),
            pltpu.VMEM((NBLK, ROWS, COLS), jnp.float32),
            pltpu.VMEM((2, COLS, EDGE), jnp.float32),
            pltpu.VMEM((2, COLS, EDGE), jnp.float32),
        ),
        in_specs=[numbers] * 3 + [away] * 6,
        out_specs=(away, away, away, away),
        scratch_shapes=[
            pltpu.VMEM((QUADS * X, ROWS, COLS), half),
            pltpu.VMEM((NBLK, ROWS, COLS), half),
            pltpu.VMEM((NBLK, ROWS, COLS), jnp.float32),
            pltpu.VMEM((2, COLS, EDGE), jnp.float32),
            pltpu.VMEM((2, COLS, EDGE), jnp.float32),
            pltpu.VMEM((NBLK + 1, ROWS, COLS), half),
            pltpu.VMEM((NBLK, ROWS, COLS), jnp.float32),
            pltpu.VMEM((8, 128), jnp.int32),
            pltpu.SMEM((8, 128), jnp.int32),
            pltpu.VMEM((NBLK, 128), jnp.int32),
            pltpu.VMEM((NBLK, 8, 128), jnp.float32),
            pltpu.VMEM((QUADS * X, ROWS, COLS), half),
            pltpu.VMEM((2, COLS, EDGE), half),
            pltpu.VMEM((2, COLS, EDGE), half),
            pltpu.VMEM((Z, Y, 2, ROWS, EDGE), half),
            pltpu.VMEM((EDGE, EDGE), half),
            pltpu.VMEM((EDGE, EDGE), half),
            pltpu.VMEM((Z, Y, 2, ROWS, HALF), half),
            pltpu.VMEM((EDGE, HALF), jnp.float32),
            pltpu.VMEM((QUADS * 2, ROWS, HALF), half),
            pltpu.VMEM((2, COLS, EDGE), half),
            pltpu.VMEM((2, COLS, EDGE), half),
            pltpu.VMEM((2, COLS, EDGE), jnp.float32),
            pltpu.VMEM((2, COLS, COLS), half),
            pltpu.VMEM((2, 2, COLS, COLS), half),
            pltpu.VMEM((14, 8, 128), jnp.float32),
            pltpu.VMEM((4, 8, 128), jnp.float32),
            pltpu.VMEM((2, 8, 128), jnp.float32),
            dma,
            dma((Y,)),
            dma,
            dma((Y,)),
            dma((2,)),
            dma,
            dma,
            dma,
            dma,
            dma((2, 2)),
            dma((2, 2)),
            dma((2,)),
            dma((2,)),
            dma((4,)),
            dma((4,)),
            dma,
            dma,
            dma,
            dma,
            dma((4,)),
            dma((6,)),
            dma,
        ],
        compiler_params=pltpu.CompilerParams(
            has_side_effects=True, vmem_limit_bytes=48 * 1024 * 1024
        ),
        cost_estimate=pl.CostEstimate(
            flops=8 * EDGE * EDGE * HALF, bytes_accessed=8 * EDGE * EDGE, transcendentals=0
        ),
    )(*[pltpu.with_memory_space_constraint(operand, pltpu.HBM) for operand in operands])


def solution(mesh):
    placed = (
        P(None, "fsdp", "group"),
        P(None, "fsdp", "group"),
        P(),
        P(),
        P(),
        P("fsdp", "group", None),
        P("fsdp", "group", None),
        P("fsdp", "group", None),
        P("fsdp", None, "group"),
    )
    return jax.shard_map(
        run_exchange,
        mesh=mesh,
        in_specs=placed,
        out_specs=(
            P(None, "fsdp", "group"),
            P(None, "fsdp", "group"),
            P("fsdp", "group", None),
            P("fsdp", "group", None),
        ),
        check_vma=False,
    )
```

time: 97.5 us -> 93.5 us (0.959); the launches traced: 95.7 us -> 93.4 us
  Pallas kernels: 95 us -> 88.4 us
  local copies, waits for them, and re-layouts: 0 us -> 4.33 us
    pallas_call x2 -> x1, Pallas kernels: 95 us -> 88.4 us  [run_exchange(): pl.pallas_call(exchange, out_shape=(pltpu.VMEM((NBLK, ROWS, COLS), half),...]
    unnamed x0 -> x4, local copies, waits for them, and re-layouts: none -> 4.33 us
where the time goes in v2:
time: 93.5 us; the launch traced here: 93.4 us
  Pallas kernels  88.4 us (95%)
  local copies, waits for them, and re-layouts  4.33 us (5%)
    pallas_call x1, Pallas kernels, run_exchange(): pl.pallas_call(exchange, out_shape=(pltpu.VMEM((NBLK, ROWS, COLS), half),...  88.4 us
    unnamed x4, local copies, waits for them, and re-layouts  4.33 us

profile of v2, /device:TPU:1, one launch (start us, length us, event | category | flops | bytes accessed | tf_op | source)
XLA Modules:
  0.0 93.4 jit_solution(7270229698954139589)
XLA Ops:
  0.6 88.4 %shard_map.120 = (bf16[56,16,256]{2,1,0:T(8,128)(2,1)S(1)}, f32[56,16,256]{2,1,0:T(8,128)S(1)}, f32[2,256,1024]{2,1,0:T(8,128)S(1)}, f32[2,256,1024]{2,1,0:T(8,128)S(1)}) custom-call(s32[56]{0:T(128)} %slot_ref.1, s32[56]{0:T(128)} %rows_ref.1, s32[56]{0:T(128)} %cols_ref.1, bf16[56,16,256]{2,1,0:T(8,128)(2,1)} %grads_ref.1, f32[56,16,256]{2,1,0:T(8,128)} %second_ref.1, ...), custom_call_target="tpu_custom_call" | custom-call | flops 4294967296 | bytes 8388608 | tf_op jit(solution)/shard_map/pallas_call | solution.py:527
  89.1 0.8 copy.17
  89.8 0.9 copy.18
  90.8 1.3 %copy.19 = f32[2,256,1024]{2,1,0:T(8,128)} copy(f32[2,256,1024]{2,1,0:T(8,128)S(1)} %get-tuple-element.6) | data formatting | bytes 4194304
  92.1 1.3 %copy.20 = f32[2,256,1024]{2,1,0:T(8,128)} copy(f32[2,256,1024]{2,1,0:T(8,128)S(1)} %get-tuple-element.7) | data formatting | bytes 4194304

commit v3 on v2

--- a/solution.py
+++ b/solution.py
@@ -115,43 +115,37 @@
     def left_block(ref, j, k):
         return ref.at[span(j), span(k)]
 
-    def send_rows():
+    def send_root(k, ff, xx, lefts, rights):
+        for d in lefts:
+            src = lroot_ref.at[k, :, span(g + d)]
+            remote(src, left_block(lroot, g, g + d), root_send.at[k], root_recv, ff, xx)
+        for d in rights:
+            src = rroot_ref.at[k, span(g + d), :]
+            remote(src, left_block(rroot, g + d, g), root_send.at[k], root_recv, ff, xx)
+
+    def send_roots():
         for k in range(2):
-
-            @pl.when(lax.rem(g - 2 * core - k + X, X) == 0)
+            home = 2 * core + k
+            around = lax.rem(g - home + X, X)
+
+            @pl.when(around == 0)
             def _():
-                for src, dst in (
-                    (lroot_ref.at[k], lroot.at[span(g)]),
-                    (rroot_ref.at[k], rroot.at[:, span(g)]),
-                ):
+                for src, dst in ((lroot_ref.at[k], lroot.at[span(g)]), (rroot_ref.at[k], rroot.at[:, span(g)])):
                     remote(src, dst, root_send.at[k], row_recv, other, g)
                     pltpu.make_async_copy(src, dst, row_recv).start()
 
-    PLAN = (
-        (1, 0, (((), (0, 1)), ((0, 1), ()), ((2,), ()))),
-        (2, 0, (((), ()), ((0,), ()), ((), ()))),
-        (2, 1, (((), (0,)), ((), ()), ((), ()))),
-        (3, 1, (((), (0, 3)), ((0,), (2,)), ((3,), ()))),
-    )
-
-    def send_roots(turn, quarter):
-        at = pl.multiple_of(quarter * 64, 64)
-        for k in range(2):
-            home = 2 * core + k
-            for steps, cc, turns in PLAN:
-                lefts, rights = turns[turn]
-                if lefts or rights:
-
-                    @pl.when(lax.rem(g - home + X, X) == steps)
-                    def _():
-                        for d in lefts:
-                            src = lroot_ref.at[k, pl.ds(at, 64), span(g + d)]
-                            dst = lroot.at[pl.ds(pl.multiple_of(g * COLS + at, 64), 64), span(g + d)]
-                            remote(src, dst, root_send.at[k], root_recv, quad * 2 + cc, home)
-                        for d in rights:
-                            row = pl.ds(pl.multiple_of(lax.rem(g + d, X) * COLS + at, 64), 64)
-                            src = rroot_ref.at[k, row, :]
-                            remote(src, rroot.at[row, span(g)], root_send.at[k], root_recv, quad * 2 + cc, home)
+            @pl.when(around == 1)
+            def _():
+                send_root(k, quad * 2, home, (0, 1, 2), (0, 1))
+
+            @pl.when(around == 2)
+            def _():
+                send_root(k, quad * 2, home, (0,), ())
+                send_root(k, quad * 2 + 1, home, (), (0,))
+
+            @pl.when(around == 3)
+            def _():
+                send_root(k, quad * 2 + 1, home, (0, 3), (0, 3, 2))
 
     load_grads = pltpu.make_async_copy(grads_ref, grads.at[pl.ds(0, NBLK)], load_sem.at[0])
     load_second = pltpu.make_async_copy(second_ref, second, load_sem.at[1])
@@ -159,6 +153,21 @@
     load_right = pltpu.make_async_copy(rstat_ref, new_right, load_sem.at[3])
     load_grads.start()
     load_second.start()
+    barrier = pltpu.get_barrier_semaphore()
+
+    def greet(ff, gg):
+        pl.semaphore_signal(barrier, inc=1, device_id=(ff, gg), device_id_type=MESH)
+
+    for d in range(X):
+        greet(other, lax.rem(g + d, X))
+        if d:
+            greet(f, lax.rem(g + d, X))
+
+    @pl.loop(1, QUADS)
+    def _(n):
+        for d in range(X):
+            greet(lax.rem(quad + n, QUADS) * 2 + core, lax.rem(g + d, X))
+
     lane = lax.broadcasted_iota(jnp.int32, (8, 128), 1)
 
     def valid(b):
@@ -183,45 +192,34 @@
         for k in range(8):
             pieces[n * 8 + k] = grads[table_smem[0, n * 8 + k]]
 
-    def send_blocks(dy):
-        yy = lax.rem(y + dy, Y)
-
-        def step(dx, carry):
-            xx = lax.rem(g + dx, X)
-            for dz in FAR_FIRST:
-                zz = lax.rem(z + dz, Z)
-                src = pieces.at[(zz * Y + yy) * X + xx]
-                to = (src, mine, block_send, block_recv.at[dy], device(zz, yy, core), xx)
-                if dy or dz:
-                    remote(*to)
-                else:
-
-                    @pl.when(dx == 0)
-                    def _():
-                        pltpu.make_async_copy(src, mine, block_recv.at[dy]).start()
-
-                    @pl.when(dx != 0)
-                    def _():
-                        remote(*to)
-
-                if dz == 2 and dy < 3:
-                    send_roots(dy, dx)
-            return carry
-
-        lax.fori_loop(0, X, step, 0)
-
-    def adam_stage(stage, first, peers):
-        for d, (ff, gg) in enumerate(peers):
-            remote(adam_sum.at[stage], adam_in.at[first + d], adam_send.at[stage], adam_recv.at[stage], ff, gg)
-
-    def adam_add(stage, first, count):
-        drain(adam_in.at[pl.ds(first, count)], adam_recv.at[stage])
-        total = adam_sum[stage]
-        for d in range(count):
-            total = total + adam_in[first + d]
-        return total
-
-    send_blocks(0)
+    pl.semaphore_wait(barrier, QUADS * X + 3)
+    send_roots()
+
+    def send_blocks(step, carry):
+        dy, dx = lax.div(step, X), lax.rem(step, X)
+        yy, xx = lax.rem(y + dy, Y), lax.rem(g + dx, X)
+        for dz in FAR_FIRST:
+            zz = lax.rem(z + dz, Z)
+            at = (zz * Y + yy) * X + xx
+            src = pieces.at[at]
+            if dz:
+                remote(src, mine, block_send, block_recv.at[dy], device(zz, yy, core), xx)
+            else:
+
+                @pl.when(step == 0)
+                def _():
+                    pltpu.make_async_copy(src, mine, block_recv.at[0]).start()
+
+                @pl.when(step != 0)
+                def _():
+                    remote(src, mine, block_send, block_recv.at[dy], device(zz, yy, core), xx)
+
+        return carry
+
+    lax.fori_loop(0, X * Y, send_blocks, 0)
+
+    load_left.start()
+    load_right.start()
 
     load_second.wait()
 
@@ -242,17 +240,18 @@
     store_moment = pltpu.make_async_copy(moments, moment_ref, store_sem.at[0])
     store_moment.start()
 
+    def adam_stage(stage, first, peers):
+        for d, (ff, gg) in enumerate(peers):
+            remote(adam_sum.at[stage], adam_in.at[first + d], adam_send.at[stage], adam_recv.at[stage], ff, gg)
+
+    def adam_add(stage, first, count):
+        drain(adam_in.at[pl.ds(first, count)], adam_recv.at[stage])
+        total = adam_sum[stage]
+        for d in range(count):
+            total = total + adam_in[first + d]
+        return total
+
     adam_stage(0, 0, [(other, g)])
-    send_blocks(1)
-    adam_sum[1] = adam_add(0, 0, 1)
-    adam_stage(1, 1, [(f, lax.rem(g + d, X)) for d in range(1, X)])
-    send_blocks(2)
-    send_rows()
-    adam_sum[2] = adam_add(1, 1, X - 1)
-    adam_stage(2, 4, [(device(z, lax.rem(y + d, Y), core), g) for d in range(1, Y)])
-    send_blocks(3)
-    load_left.start()
-    load_right.start()
 
     def pass_on(ref, j, k):
         here = left_block(ref, j, k)
@@ -270,8 +269,8 @@
         for ref, j, k in ((lroot, 3, 3), (lroot, 3, 2), (rroot, 3, 3), (rroot, 2, 3), (rroot, 1, 3), (rroot, 2, 2)):
             pass_on(ref, g + j, g + k)
 
-    adam_sum[3] = adam_add(2, 4, Y - 1)
-    adam_stage(3, 7, [(device(lax.rem(z + d, Z), y, core), g) for d in range(1, Z)])
+    adam_sum[1] = adam_add(0, 0, 1)
+    adam_stage(1, 1, [(f, lax.rem(g + d, X)) for d in range(1, X)])
 
     drain(lroot.at[pl.ds(0, 2 * COLS)], row_recv)
     drain(lroot.at[pl.ds(0, 6 * COLS // X)], pass_recv)
@@ -281,28 +280,24 @@
         lroot[span(g + k), span(g + j)] = lroot[span(g + j), span(g + k)].T
     half = pl.ds(pl.multiple_of(core * HALF, HALF), HALF)
 
-    def send_gram(which, m, src, dst, at, size):
+    def send_gram(which, m, src, dst):
         xx = 2 * core + m
         ff = quad * 2 + side
         around = lax.rem(xx - g + X, X)
         send = gram_send.at[which, m]
-        rows = pl.ds(at if isinstance(at, int) else pl.multiple_of(at, 16), size)
 
         @pl.when(around == 0)
         def _():
-            here, there = src.at[m, rows], dst.at[parity, rows]
-            pltpu.make_async_copy(here, there, gram_recv.at[which, parity]).start()
+            pltpu.make_async_copy(src.at[m], dst.at[parity], gram_recv.at[which, parity]).start()
 
         @pl.when(lax.rem(around, 2) == 1)
         def _():
-            here, there = src.at[m, rows], dst.at[parity, rows]
-            remote(here, there, send, gram_recv.at[which, parity], ff, xx)
+            remote(src.at[m], dst.at[parity], send, gram_recv.at[which, parity], ff, xx)
 
         @pl.when(around == 2)
         def _():
             for d, gg in ((0, lax.rem(g + 1, X)), (2, lax.rem(g + 3, X))):
-                here = src.at[m, rows, span(g + d)]
-                remote(here, relay.at[which, rows], send, relay_recv.at[which], ff, gg)
+                remote(src.at[m, :, span(g + d)], relay.at[which], send, relay_recv.at[which], ff, gg)
 
     def swap(d):
         ys = lax.rem(y + Y - d, Y)
@@ -327,7 +322,7 @@
                 gram_part[m] = value
             else:
                 gright[m] = value.astype(jnp.bfloat16)
-                send_gram(1, m, gright, gright_in, 0, 128)
+                send_gram(1, m, gright, gright_in)
         value = jnp.dot(
             block[:, ys].reshape(COLS, EDGE), rroot[:, half], preferred_element_type=jnp.float32
         )
@@ -342,6 +337,9 @@
     group(2)
     group(3)
 
+    adam_sum[2] = adam_add(1, 1, X - 1)
+    adam_stage(2, 4, [(device(z, lax.rem(y + d, Y), core), g) for d in range(1, Y)])
+
     rows_valid, cols_valid = 0, 0
     for b in range(NBLK):
         rows_valid = jnp.where(slot_ref[b] == slot, rows_ref[b], rows_valid)
@@ -361,6 +359,9 @@
     norm[0] = jnp.broadcast_to(jnp.sum(total, keepdims=True), (8, 128))
     remote(norm.at[0], norm.at[1], norm_send, norm_recv, other, g)
 
+    adam_sum[3] = adam_add(2, 4, Y - 1)
+    adam_stage(3, 7, [(device(lax.rem(z + d, Z), y, core), g) for d in range(1, Z)])
+
     for m in range(2):
         gleft[m] = lax.dot_general(
             block[pl.ds(core * 4 + m * 2, 2)].reshape(COLS, EDGE),
@@ -368,6 +369,7 @@
             (((1,), (1,)), ((), ())),
             preferred_element_type=jnp.float32,
         ).astype(jnp.bfloat16)
+        send_gram(0, m, gleft, gleft_in)
 
     adam = adam_add(3, 7, Z - 1)
     adam = jnp.sum(jnp.where(lane == slot, adam, 0.0)[0:1], keepdims=True)
@@ -401,17 +403,6 @@
                 @pl.when(jnp.logical_not(local))
                 def _():
                     remote(src, dst, out_send, out_recv, ff, xx)
-
-            if dz in (3, 6):
-                m = 0 if dz == 3 else 1
-                send_gram(0, m, gleft, gleft_in, step * 16, 16)
-
-            if dz in (2, 7):
-                m = 0 if dz == 2 else 1
-
-                @pl.when(lax.rem(step, 2) == 0)
-                def _():
-                    send_gram(1, m, gright, gright_in, 128 + step * 8, 16)
 
         return carry
 
@@ -587,7 +578,7 @@
             dma,
         ],
         compiler_params=pltpu.CompilerParams(
-            has_side_effects=True, vmem_limit_bytes=48 * 1024 * 1024
+            collective_id=0, has_side_effects=True, vmem_limit_bytes=48 * 1024 * 1024
         ),
         cost_estimate=pl.CostEstimate(
             flops=8 * EDGE * EDGE * HALF, bytes_accessed=8 * EDGE * EDGE, transcendentals=0

time: 93.5 us -> 83.3 us (0.89)
  Pallas kernels: 88.4 us -> 78.2 us
    pallas_call x1, Pallas kernels: 88.4 us -> 78.2 us  [run_exchange(): pl.pallas_call(exchange, out_shape=(pltpu.VMEM((NBLK, ROWS, COLS), half),...]
where the time goes in v3:
time: 83.3 us; the launch traced here: 83.2 us
  Pallas kernels  78.2 us (94%)
  local copies, waits for them, and re-layouts  4.33 us (5%)
    pallas_call x1, Pallas kernels, run_exchange(): pl.pallas_call(exchange, out_shape=(pltpu.VMEM((NBLK, ROWS, COLS), half),...  78.2 us
    unnamed x4, local copies, waits for them, and re-layouts  4.33 us

profile of v3, /device:TPU:1, one launch (start us, length us, event | category | flops | bytes accessed | tf_op | source)
XLA Modules:
  0.0 83.2 jit_solution(6727103305430871965)
XLA Ops:
  0.6 78.2 %shard_map.120 = (bf16[56,16,256]{2,1,0:T(8,128)(2,1)S(1)}, f32[56,16,256]{2,1,0:T(8,128)S(1)}, f32[2,256,1024]{2,1,0:T(8,128)S(1)}, f32[2,256,1024]{2,1,0:T(8,128)S(1)}) custom-call(s32[56]{0:T(128)} %slot_ref.1, s32[56]{0:T(128)} %rows_ref.1, s32[56]{0:T(128)} %cols_ref.1, bf16[56,16,256]{2,1,0:T(8,128)(2,1)} %grads_ref.1, f32[56,16,256]{2,1,0:T(8,128)} %second_ref.1, ...), custom_call_target="tpu_custom_call" | custom-call | flops 4294967296 | bytes 8388608 | tf_op jit(solution)/shard_map/pallas_call | solution.py:518
  78.9 0.8 copy.17
  79.6 0.9 %copy.18 = f32[56,16,256]{2,1,0:T(8,128)} copy(f32[56,16,256]{2,1,0:T(8,128)S(1)} %get-tuple-element.5) | data formatting | bytes 1835008
  80.6 1.3 %copy.19 = f32[2,256,1024]{2,1,0:T(8,128)} copy(f32[2,256,1024]{2,1,0:T(8,128)S(1)} %get-tuple-element.6) | data formatting | bytes 4194304
  81.9 1.3 %copy.20 = f32[2,256,1024]{2,1,0:T(8,128)} copy(f32[2,256,1024]{2,1,0:T(8,128)S(1)} %get-tuple-element.7) | data formatting | bytes 4194304

commit v4 on v3

--- a/solution.py
+++ b/solution.py
@@ -29,15 +29,11 @@
     rstat_ref,
     lroot_ref,
     rroot_ref,
-    directions_ref,
-    moment_ref,
-    new_left_ref,
-    new_right_ref,
-    returned,
     directions,
     moments,
     new_left,
     new_right,
+    returned,
     grads,
     second,
     table,
@@ -81,8 +77,8 @@
     out_send,
     out_recv,
     load_sem,
-    store_sem,
     table_sem,
+    ready,
 ):
     f = lax.axis_index("fsdp")
     g = lax.axis_index("group")
@@ -154,19 +150,18 @@
     load_grads.start()
     load_second.start()
     barrier = pltpu.get_barrier_semaphore()
-
-    def greet(ff, gg):
-        pl.semaphore_signal(barrier, inc=1, device_id=(ff, gg), device_id_type=MESH)
-
-    for d in range(X):
-        greet(other, lax.rem(g + d, X))
-        if d:
-            greet(f, lax.rem(g + d, X))
-
-    @pl.loop(1, QUADS)
-    def _(n):
-        for d in range(X):
-            greet(lax.rem(quad + n, QUADS) * 2 + core, lax.rem(g + d, X))
+    along_z = [device(lax.rem(z + d, Z), y, core) for d in range(1, Z)]
+
+    def greet(sem, ff, gg):
+        pl.semaphore_signal(sem, inc=1, device_id=(ff, gg), device_id_type=MESH)
+
+    for ff in along_z:
+        greet(barrier, ff, g)
+    for dx in range(X):
+        greet(barrier, other, lax.rem(g + dx, X))
+        for dy in range(Y):
+            if dx or dy:
+                greet(barrier, device(z, lax.rem(y + dy, Y), core), lax.rem(g + dx, X))
 
     lane = lax.broadcasted_iota(jnp.int32, (8, 128), 1)
 
@@ -182,6 +177,10 @@
     to_smem = pltpu.make_async_copy(table, table_smem, table_sem)
     to_smem.start()
     grads[NBLK] = jnp.zeros((ROWS, COLS), jnp.bfloat16)
+    pl.semaphore_wait(barrier, X * Y - 1 + Z - 1 + X)
+    for ff in along_z:
+        greet(ready, ff, g)
+    send_roots()
     to_smem.wait()
     load_grads.wait()
 
@@ -192,8 +191,7 @@
         for k in range(8):
             pieces[n * 8 + k] = grads[table_smem[0, n * 8 + k]]
 
-    pl.semaphore_wait(barrier, QUADS * X + 3)
-    send_roots()
+    pl.semaphore_wait(ready, Z - 1)
 
     def send_blocks(step, carry):
         dy, dx = lax.div(step, X), lax.rem(step, X)
@@ -237,8 +235,6 @@
     adam = jnp.sum(jnp.sum(adam_parts[...], axis=1), axis=1, keepdims=True)
     adam = jnp.where(matches[...] != 0, adam, 0.0)
     adam_sum[0] = jnp.broadcast_to(jnp.sum(adam, axis=0, keepdims=True), (8, 128))
-    store_moment = pltpu.make_async_copy(moments, moment_ref, store_sem.at[0])
-    store_moment.start()
 
     def adam_stage(stage, first, peers):
         for d, (ff, gg) in enumerate(peers):
@@ -431,13 +427,11 @@
             at = pl.ds(pl.multiple_of(m * 32, 32), 32)
             target[k, at] = 0.9 * target[k, at] + 0.1 * gram[k, at].astype(jnp.float32)
 
-    store_left = [pltpu.make_async_copy(new_left.at[k], new_left_ref.at[k], store_sem.at[1 + k]) for k in range(2)]
-    store_right = [pltpu.make_async_copy(new_right.at[k], new_right_ref.at[k], store_sem.at[3 + k]) for k in range(2)]
-    parts = ((1, new_right, gright_in, store_right), (0, new_left, gleft_in, store_left))
+    parts = ((1, new_right, gright_in), (0, new_left, gleft_in))
     load_left.wait()
     load_right.wait()
     for last in (False, True):
-        for which, target, gram, store in parts:
+        for which, target, gram in parts:
             for k in range(2):
 
                 @pl.when((arounds[k] == 2) == last)
@@ -453,7 +447,6 @@
                             drain(gram.at[k], gram_recv.at[which, k])
 
                     update(target, gram, k)
-                    store[k].start()
 
     drain(pieces.at[pl.ds(0, QUADS * X - 1)], block_send)
     drain(pieces, swap_send)
@@ -500,18 +493,12 @@
         return carry
 
     lax.fori_loop(0, NBLK, one_direction, 0, unroll=8)
-    store_directions = pltpu.make_async_copy(directions, directions_ref, store_sem.at[5])
-    store_directions.start()
-    store_directions.wait()
-
-    store_moment.wait()
-    for store in store_left + store_right:
-        store.wait()
 
 
 def run_exchange(grads, second_moment, slot_of, block_rows, block_cols, *matrices):
     half = jnp.bfloat16
     away = pl.BlockSpec(memory_space=pl.ANY)
+    here = pl.BlockSpec(memory_space=pltpu.VMEM)
     numbers = pl.BlockSpec(memory_space=pltpu.SMEM)
     dma = pltpu.SemaphoreType.DMA
     operands = (slot_of, block_rows, block_cols, grads, second_moment, *matrices)
@@ -524,13 +511,9 @@
             pltpu.VMEM((2, COLS, EDGE), jnp.float32),
         ),
         in_specs=[numbers] * 3 + [away] * 6,
-        out_specs=(away, away, away, away),
+        out_specs=(here,) * 4,
         scratch_shapes=[
             pltpu.VMEM((QUADS * X, ROWS, COLS), half),
-            pltpu.VMEM((NBLK, ROWS, COLS), half),
-            pltpu.VMEM((NBLK, ROWS, COLS), jnp.float32),
-            pltpu.VMEM((2, COLS, EDGE), jnp.float32),
-            pltpu.VMEM((2, COLS, EDGE), jnp.float32),
             pltpu.VMEM((NBLK + 1, ROWS, COLS), half),
             pltpu.VMEM((NBLK, ROWS, COLS), jnp.float32),
             pltpu.VMEM((8, 128), jnp.int32),
@@ -574,8 +557,8 @@
             dma,
             dma,
             dma((4,)),
-            dma((6,)),
-            dma,
+            dma,
+            pltpu.SemaphoreType.REGULAR,
         ],
         compiler_params=pltpu.CompilerParams(
             collective_id=0, has_side_effects=True, vmem_limit_bytes=48 * 1024 * 1024

time: 83.3 us -> 82.6 us (level)
  no operation moved by 1% of the time
where the time goes in v4:
time: 82.6 us; the launch traced here: 82.5 us
  Pallas kernels  77.5 us (94%)
  local copies, waits for them, and re-layouts  4.33 us (5%)
    pallas_call x1, Pallas kernels, run_exchange(): pl.pallas_call(exchange, out_shape=(pltpu.VMEM((NBLK, ROWS, COLS), half),...  77.5 us
    unnamed x4, local copies, waits for them, and re-layouts  4.33 us

profile of v4, /device:TPU:1, one launch (start us, length us, event | category | flops | bytes accessed | tf_op | source)
XLA Modules:
  0.0 82.5 jit_solution(6095727115165405885)
XLA Ops:
  0.6 77.5 %shard_map.120 = (bf16[56,16,256]{2,1,0:T(8,128)(2,1)S(1)}, f32[56,16,256]{2,1,0:T(8,128)S(1)}, f32[2,256,1024]{2,1,0:T(8,128)S(1)}, f32[2,256,1024]{2,1,0:T(8,128)S(1)}) custom-call(s32[56]{0:T(128)} %slot_ref.1, s32[56]{0:T(128)} %rows_ref.1, s32[56]{0:T(128)} %cols_ref.1, bf16[56,16,256]{2,1,0:T(8,128)(2,1)} %grads_ref.1, f32[56,16,256]{2,1,0:T(8,128)} %second_ref.1, ...), custom_call_target="tpu_custom_call" | custom-call | flops 4294967296 | bytes 8388608 | tf_op jit(solution)/shard_map/pallas_call | solution.py:505
  78.2 0.8 copy.17
  78.9 0.9 %copy.18 = f32[56,16,256]{2,1,0:T(8,128)} copy(f32[56,16,256]{2,1,0:T(8,128)S(1)} %get-tuple-element.5) | data formatting | bytes 1835008
  79.9 1.3 %copy.19 = f32[2,256,1024]{2,1,0:T(8,128)} copy(f32[2,256,1024]{2,1,0:T(8,128)S(1)} %get-tuple-element.6) | data formatting | bytes 4194304
  81.2 1.3 %copy.20 = f32[2,256,1024]{2,1,0:T(8,128)} copy(f32[2,256,1024]{2,1,0:T(8,128)S(1)} %get-tuple-element.7) | data formatting | bytes 4194304

commit v5 on v4

--- a/solution.py
+++ b/solution.py
@@ -78,7 +78,6 @@
     out_recv,
     load_sem,
     table_sem,
-    ready,
 ):
     f = lax.axis_index("fsdp")
     g = lax.axis_index("group")
@@ -150,18 +149,19 @@
     load_grads.start()
     load_second.start()
     barrier = pltpu.get_barrier_semaphore()
-    along_z = [device(lax.rem(z + d, Z), y, core) for d in range(1, Z)]
-
-    def greet(sem, ff, gg):
-        pl.semaphore_signal(sem, inc=1, device_id=(ff, gg), device_id_type=MESH)
-
-    for ff in along_z:
-        greet(barrier, ff, g)
-    for dx in range(X):
-        greet(barrier, other, lax.rem(g + dx, X))
-        for dy in range(Y):
-            if dx or dy:
-                greet(barrier, device(z, lax.rem(y + dy, Y), core), lax.rem(g + dx, X))
+
+    def greet(ff, gg):
+        pl.semaphore_signal(barrier, inc=1, device_id=(ff, gg), device_id_type=MESH)
+
+    for d in range(X):
+        greet(other, lax.rem(g + d, X))
+        if d:
+            greet(f, lax.rem(g + d, X))
+
+    @pl.loop(1, QUADS)
+    def _(n):
+        for d in range(X):
+            greet(lax.rem(quad + n, QUADS) * 2 + core, lax.rem(g + d, X))
 
     lane = lax.broadcasted_iota(jnp.int32, (8, 128), 1)
 
@@ -177,10 +177,6 @@
     to_smem = pltpu.make_async_copy(table, table_smem, table_sem)
     to_smem.start()
     grads[NBLK] = jnp.zeros((ROWS, COLS), jnp.bfloat16)
-    pl.semaphore_wait(barrier, X * Y - 1 + Z - 1 + X)
-    for ff in along_z:
-        greet(ready, ff, g)
-    send_roots()
     to_smem.wait()
     load_grads.wait()
 
@@ -191,7 +187,8 @@
         for k in range(8):
             pieces[n * 8 + k] = grads[table_smem[0, n * 8 + k]]
 
-    pl.semaphore_wait(ready, Z - 1)
+    pl.semaphore_wait(barrier, QUADS * X + 3)
+    send_roots()
 
     def send_blocks(step, carry):
         dy, dx = lax.div(step, X), lax.rem(step, X)
@@ -253,27 +250,6 @@
         here = left_block(ref, j, k)
         remote(here, here, pass_send, pass_recv, other, g)
 
-    drain(lroot.at[pl.ds(0, 6 * COLS // X)], root_recv)
-
-    @pl.when(core == 0)
-    def _():
-        for ref, j, k in ((lroot, 1, 1), (lroot, 1, 2), (lroot, 1, 3), (lroot, 2, 2), (rroot, 1, 1), (rroot, 2, 1)):
-            pass_on(ref, g + j, g + k)
-
-    @pl.when(core == 1)
-    def _():
-        for ref, j, k in ((lroot, 3, 3), (lroot, 3, 2), (rroot, 3, 3), (rroot, 2, 3), (rroot, 1, 3), (rroot, 2, 2)):
-            pass_on(ref, g + j, g + k)
-
-    adam_sum[1] = adam_add(0, 0, 1)
-    adam_stage(1, 1, [(f, lax.rem(g + d, X)) for d in range(1, X)])
-
-    drain(lroot.at[pl.ds(0, 2 * COLS)], row_recv)
-    drain(lroot.at[pl.ds(0, 6 * COLS // X)], pass_recv)
-    for j, k in ((1, 0), (2, 0), (3, 0), (2, 1), (2, 3), (1, 3)):
-        rroot[span(g + k), span(g + j)] = rroot[span(g + j), span(g + k)].T
-    for j, k in ((0, 1), (0, 2), (0, 3), (1, 2), (3, 2), (1, 3)):
-        lroot[span(g + k), span(g + j)] = lroot[span(g + j), span(g + k)].T
     half = pl.ds(pl.multiple_of(core * HALF, HALF), HALF)
 
     def send_gram(which, m, src, dst):
@@ -301,7 +277,7 @@
         drain(rows, block_recv.at[d])
         remote(rows, rows, swap_send, swap_recv.at[d], other, g)
 
-    def group(d):
+    def gram(d):
         ys = lax.rem(y + Y - d, Y)
         drain(block.at[:, ys, 1 - core], swap_recv.at[d])
         for m in range(2):
@@ -319,6 +295,9 @@
             else:
                 gright[m] = value.astype(jnp.bfloat16)
                 send_gram(1, m, gright, gright_in)
+
+    def mix(d):
+        ys = lax.rem(y + Y - d, Y)
         value = jnp.dot(
             block[:, ys].reshape(COLS, EDGE), rroot[:, half], preferred_element_type=jnp.float32
         )
@@ -326,15 +305,42 @@
 
     swap(0)
     swap(1)
-    group(0)
+    gram(0)
+
+    drain(lroot.at[pl.ds(0, 6 * COLS // X)], root_recv)
+
+    @pl.when(core == 0)
+    def _():
+        for ref, j, k in ((lroot, 1, 1), (lroot, 1, 2), (lroot, 1, 3), (lroot, 2, 2), (rroot, 1, 1), (rroot, 2, 1)):
+            pass_on(ref, g + j, g + k)
+
+    @pl.when(core == 1)
+    def _():
+        for ref, j, k in ((lroot, 3, 3), (lroot, 3, 2), (rroot, 3, 3), (rroot, 2, 3), (rroot, 1, 3), (rroot, 2, 2)):
+            pass_on(ref, g + j, g + k)
+
+    adam_sum[1] = adam_add(0, 0, 1)
+    adam_stage(1, 1, [(f, lax.rem(g + d, X)) for d in range(1, X)])
+    gram(1)
+
+    drain(lroot.at[pl.ds(0, 2 * COLS)], row_recv)
+    drain(lroot.at[pl.ds(0, 6 * COLS // X)], pass_recv)
+    for j, k in ((1, 0), (2, 0), (3, 0), (2, 1), (2, 3), (1, 3)):
+        rroot[span(g + k), span(g + j)] = rroot[span(g + j), span(g + k)].T
+    for j, k in ((0, 1), (0, 2), (0, 3), (1, 2), (3, 2), (1, 3)):
+        lroot[span(g + k), span(g + j)] = lroot[span(g + j), span(g + k)].T
+
     swap(2)
-    group(1)
-    swap(3)
-    group(2)
-    group(3)
-
+    gram(2)
     adam_sum[2] = adam_add(1, 1, X - 1)
     adam_stage(2, 4, [(device(z, lax.rem(y + d, Y), core), g) for d in range(1, Y)])
+    swap(3)
+    for d in range(3):
+        mix(d)
+    gram(3)
+    mix(3)
+    adam_sum[3] = adam_add(2, 4, Y - 1)
+    adam_stage(3, 7, [(device(lax.rem(z + d, Z), y, core), g) for d in range(1, Z)])
 
     rows_valid, cols_valid = 0, 0
     for b in range(NBLK):
@@ -354,9 +360,6 @@
     total = lax.fori_loop(0, 4, one_part, jnp.zeros((8, HALF), jnp.float32))
     norm[0] = jnp.broadcast_to(jnp.sum(total, keepdims=True), (8, 128))
     remote(norm.at[0], norm.at[1], norm_send, norm_recv, other, g)
-
-    adam_sum[3] = adam_add(2, 4, Y - 1)
-    adam_stage(3, 7, [(device(lax.rem(z + d, Z), y, core), g) for d in range(1, Z)])
 
     for m in range(2):
         gleft[m] = lax.dot_general(
@@ -558,7 +561,6 @@
             dma,
             dma((4,)),
             dma,
-            pltpu.SemaphoreType.REGULAR,
         ],
         compiler_params=pltpu.CompilerParams(
             collective_id=0, has_side_effects=True, vmem_limit_bytes=48 * 1024 * 1024

time: 82.6 us -> 84.3 us (1.021)
  Pallas kernels: 77.5 us -> 79.2 us
    pallas_call x1, Pallas kernels: 77.5 us -> 79.2 us  [run_exchange(): pl.pallas_call(exchange, out_shape=(pltpu.VMEM((NBLK, ROWS, COLS), half),...]
where the time goes in v5:
time: 84.3 us; the launch traced here: 84.2 us
  Pallas kernels  79.2 us (94%)
  local copies, waits for them, and re-layouts  4.33 us (5%)
    pallas_call x1, Pallas kernels, run_exchange(): pl.pallas_call(exchange, out_shape=(pltpu.VMEM((NBLK, ROWS, COLS), half),...  79.2 us
    unnamed x4, local copies, waits for them, and re-layouts  4.33 us

profile of v5, /device:TPU:1, one launch (start us, length us, event | category | flops | bytes accessed | tf_op | source)
XLA Modules:
  0.0 84.2 jit_solution(10266906833377286939)
XLA Ops:
  0.6 79.2 %shard_map.120 = (bf16[56,16,256]{2,1,0:T(8,128)(2,1)S(1)}, f32[56,16,256]{2,1,0:T(8,128)S(1)}, f32[2,256,1024]{2,1,0:T(8,128)S(1)}, f32[2,256,1024]{2,1,0:T(8,128)S(1)}) custom-call(s32[56]{0:T(128)} %slot_ref.1, s32[56]{0:T(128)} %rows_ref.1, s32[56]{0:T(128)} %cols_ref.1, bf16[56,16,256]{2,1,0:T(8,128)(2,1)} %grads_ref.1, f32[56,16,256]{2,1,0:T(8,128)} %second_ref.1, ...), custom_call_target="tpu_custom_call" | custom-call | flops 4294967296 | bytes 8388608 | tf_op jit(solution)/shard_map/pallas_call | solution.py:508
  79.9 0.8 copy.17
  80.7 0.9 %copy.18 = f32[56,16,256]{2,1,0:T(8,128)} copy(f32[56,16,256]{2,1,0:T(8,128)S(1)} %get-tuple-element.5) | data formatting | bytes 1835008
  81.6 1.3 %copy.19 = f32[2,256,1024]{2,1,0:T(8,128)} copy(f32[2,256,1024]{2,1,0:T(8,128)S(1)} %get-tuple-element.6) | data formatting | bytes 4194304
  82.9 1.3 %copy.20 = f32[2,256,1024]{2,1,0:T(8,128)} copy(f32[2,256,1024]{2,1,0:T(8,128)S(1)} %get-tuple-element.7) | data formatting | bytes 4194304

commit v6 on v5

--- a/solution.py
+++ b/solution.py
@@ -498,6 +498,19 @@
     lax.fori_loop(0, NBLK, one_direction, 0, unroll=8)
 
 
+def hand_over(*refs):
+    count = (len(refs) - 1) // 2
+    sems = refs[-1]
+    copies = [
+        pltpu.make_async_copy(src, dst, sems.at[n])
+        for n, (src, dst) in enumerate(zip(refs[:count], refs[count : 2 * count]))
+    ]
+    for copy in copies:
+        copy.start()
+    for copy in copies:
+        copy.wait()
+
+
 def run_exchange(grads, second_moment, slot_of, block_rows, block_cols, *matrices):
     half = jnp.bfloat16
     away = pl.BlockSpec(memory_space=pl.ANY)
@@ -505,13 +518,13 @@
     numbers = pl.BlockSpec(memory_space=pltpu.SMEM)
     dma = pltpu.SemaphoreType.DMA
     operands = (slot_of, block_rows, block_cols, grads, second_moment, *matrices)
-    return pl.pallas_call(
+    results = pl.pallas_call(
         exchange,
         out_shape=(
-            pltpu.VMEM((NBLK, ROWS, COLS), half),
-            pltpu.VMEM((NBLK, ROWS, COLS), jnp.float32),
-            pltpu.VMEM((2, COLS, EDGE), jnp.float32),
-            pltpu.VMEM((2, COLS, EDGE), jnp.float32),
+            jax.ShapeDtypeStruct((NBLK, ROWS, COLS), half),
+            jax.ShapeDtypeStruct((NBLK, ROWS, COLS), jnp.float32),
+            jax.ShapeDtypeStruct((2, COLS, EDGE), jnp.float32),
+            jax.ShapeDtypeStruct((2, COLS, EDGE), jnp.float32),
         ),
         in_specs=[numbers] * 3 + [away] * 6,
         out_specs=(here,) * 4,
@@ -569,6 +582,14 @@
             flops=8 * EDGE * EDGE * HALF, bytes_accessed=8 * EDGE * EDGE, transcendentals=0
         ),
     )(*[pltpu.with_memory_space_constraint(operand, pltpu.HBM) for operand in operands])
+    return pl.pallas_call(
+        hand_over,
+        out_shape=[jax.ShapeDtypeStruct(result.shape, result.dtype) for result in results],
+        in_specs=[here] * len(results),
+        out_specs=[away] * len(results),
+        scratch_shapes=[dma((len(results),))],
+        compiler_params=pltpu.CompilerParams(vmem_limit_bytes=16 * 1024 * 1024),
+    )(*results)
 
 
 def solution(mesh):

time: 84.3 us -> 82.5 us (0.979)
  local copies, waits for them, and re-layouts: 4.33 us -> 0 us
  Pallas kernels: 79.2 us -> 81.7 us
    unnamed x4 -> x0, local copies, waits for them, and re-layouts: 4.33 us -> none
    pallas_call x1 -> x2, Pallas kernels: 79.2 us -> 81.7 us  [the longest x1 79.2 us: run_exchange(): pl.pallas_call(exchange, out_shape=(jax.ShapeDtypeStruct((NBLK, ROWS, COL...]
where the time goes in v6:
time: 82.5 us; the launch traced here: 82.4 us
  Pallas kernels  81.7 us (99%)
    pallas_call x1, Pallas kernels, run_exchange(): pl.pallas_call(exchange, out_shape=(jax.ShapeDtypeStruct((NBLK, ROWS, COL...  79.2 us
    pallas_call x1, Pallas kernels, run_exchange(): pl.pallas_call(hand_over, out_shape=[jax.ShapeDtypeStruct(result.shape, r...  2.5 us

profile of v6, /device:TPU:1, one launch (start us, length us, event | category | flops | bytes accessed | tf_op | source)
XLA Modules:
  0.0 82.4 jit_solution(3829215599610867883)
XLA Ops:
  0.6 79.2 %shard_map.120 = (bf16[56,16,256]{2,1,0:T(8,128)(2,1)S(1)}, f32[56,16,256]{2,1,0:T(8,128)S(1)}, f32[2,256,1024]{2,1,0:T(8,128)S(1)}, f32[2,256,1024]{2,1,0:T(8,128)S(1)}) custom-call(s32[56]{0:T(128)} %slot_ref.1, s32[56]{0:T(128)} %rows_ref.1, s32[56]{0:T(128)} %cols_ref.1, bf16[56,16,256]{2,1,0:T(8,128)(2,1)} %grads_ref.1, f32[56,16,256]{2,1,0:T(8,128)} %second_ref.1, ...), custom_call_target="tpu_custom_call" | custom-call | flops 4294967296 | bytes 8388608 | tf_op jit(solution)/shard_map/pallas_call | solution.py:521
  79.9 2.5 %shard_map.121 = (bf16[56,16,256]{2,1,0:T(8,128)(2,1)}, f32[56,16,256]{2,1,0:T(8,128)}, f32[2,256,1024]{2,1,0:T(8,128)}, f32[2,256,1024]{2,1,0:T(8,128)}) custom-call(bf16[56,16,256]{2,1,0:T(8,128)(2,1)S(1)} %get-tuple-element.8.refs_0_, f32[56,16,256]{2,1,0:T(8,128)S(1)} %get-tuple-element.9.refs_1_, f32[2,256,1024]{2,1,0:T(8,128)S(1)} %get-tuple-element.10.refs_2_, ...), custom_call_target="tpu_custom_call" | custom-call | tf_op jit(solution)/shard_map/pallas_call | solution.py:585

commit v7 on v6

--- a/solution.py
+++ b/solution.py
@@ -250,6 +250,27 @@
         here = left_block(ref, j, k)
         remote(here, here, pass_send, pass_recv, other, g)
 
+    drain(lroot.at[pl.ds(0, 6 * COLS // X)], root_recv)
+
+    @pl.when(core == 0)
+    def _():
+        for ref, j, k in ((lroot, 1, 1), (lroot, 1, 2), (lroot, 1, 3), (lroot, 2, 2), (rroot, 1, 1), (rroot, 2, 1)):
+            pass_on(ref, g + j, g + k)
+
+    @pl.when(core == 1)
+    def _():
+        for ref, j, k in ((lroot, 3, 3), (lroot, 3, 2), (rroot, 3, 3), (rroot, 2, 3), (rroot, 1, 3), (rroot, 2, 2)):
+            pass_on(ref, g + j, g + k)
+
+    adam_sum[1] = adam_add(0, 0, 1)
+    adam_stage(1, 1, [(f, lax.rem(g + d, X)) for d in range(1, X)])
+
+    drain(lroot.at[pl.ds(0, 2 * COLS)], row_recv)
+    drain(lroot.at[pl.ds(0, 6 * COLS // X)], pass_recv)
+    for j, k in ((1, 0), (2, 0), (3, 0), (2, 1), (2, 3), (1, 3)):
+        rroot[span(g + k), span(g + j)] = rroot[span(g + j), span(g + k)].T
+    for j, k in ((0, 1), (0, 2), (0, 3), (1, 2), (3, 2), (1, 3)):
+        lroot[span(g + k), span(g + j)] = lroot[span(g + j), span(g + k)].T
     half = pl.ds(pl.multiple_of(core * HALF, HALF), HALF)
 
     def send_gram(which, m, src, dst):
@@ -277,7 +298,7 @@
         drain(rows, block_recv.at[d])
         remote(rows, rows, swap_send, swap_recv.at[d], other, g)
 
-    def gram(d):
+    def group(d):
         ys = lax.rem(y + Y - d, Y)
         drain(block.at[:, ys, 1 - core], swap_recv.at[d])
         for m in range(2):
@@ -295,9 +316,6 @@
             else:
                 gright[m] = value.astype(jnp.bfloat16)
                 send_gram(1, m, gright, gright_in)
-
-    def mix(d):
-        ys = lax.rem(y + Y - d, Y)
         value = jnp.dot(
             block[:, ys].reshape(COLS, EDGE), rroot[:, half], preferred_element_type=jnp.float32
         )
@@ -305,42 +323,15 @@
 
     swap(0)
     swap(1)
-    gram(0)
-
-    drain(lroot.at[pl.ds(0, 6 * COLS // X)], root_recv)
-
-    @pl.when(core == 0)
-    def _():
-        for ref, j, k in ((lroot, 1, 1), (lroot, 1, 2), (lroot, 1, 3), (lroot, 2, 2), (rroot, 1, 1), (rroot, 2, 1)):
-            pass_on(ref, g + j, g + k)
-
-    @pl.when(core == 1)
-    def _():
-        for ref, j, k in ((lroot, 3, 3), (lroot, 3, 2), (rroot, 3, 3), (rroot, 2, 3), (rroot, 1, 3), (rroot, 2, 2)):
-            pass_on(ref, g + j, g + k)
-
-    adam_sum[1] = adam_add(0, 0, 1)
-    adam_stage(1, 1, [(f, lax.rem(g + d, X)) for d in range(1, X)])
-    gram(1)
-
-    drain(lroot.at[pl.ds(0, 2 * COLS)], row_recv)
-    drain(lroot.at[pl.ds(0, 6 * COLS // X)], pass_recv)
-    for j, k in ((1, 0), (2, 0), (3, 0), (2, 1), (2, 3), (1, 3)):
-        rroot[span(g + k), span(g + j)] = rroot[span(g + j), span(g + k)].T
-    for j, k in ((0, 1), (0, 2), (0, 3), (1, 2), (3, 2), (1, 3)):
-        lroot[span(g + k), span(g + j)] = lroot[span(g + j), span(g + k)].T
-
+    group(0)
     swap(2)
-    gram(2)
+    group(1)
+    swap(3)
+    group(2)
+    group(3)
+
     adam_sum[2] = adam_add(1, 1, X - 1)
     adam_stage(2, 4, [(device(z, lax.rem(y + d, Y), core), g) for d in range(1, Y)])
-    swap(3)
-    for d in range(3):
-        mix(d)
-    gram(3)
-    mix(3)
-    adam_sum[3] = adam_add(2, 4, Y - 1)
-    adam_stage(3, 7, [(device(lax.rem(z + d, Z), y, core), g) for d in range(1, Z)])
 
     rows_valid, cols_valid = 0, 0
     for b in range(NBLK):
@@ -360,6 +351,9 @@
     total = lax.fori_loop(0, 4, one_part, jnp.zeros((8, HALF), jnp.float32))
     norm[0] = jnp.broadcast_to(jnp.sum(total, keepdims=True), (8, 128))
     remote(norm.at[0], norm.at[1], norm_send, norm_recv, other, g)
+
+    adam_sum[3] = adam_add(2, 4, Y - 1)
+    adam_stage(3, 7, [(device(lax.rem(z + d, Z), y, core), g) for d in range(1, Z)])
 
     for m in range(2):
         gleft[m] = lax.dot_general(

time: 82.5 us -> 81.1 us (0.983)
  Pallas kernels: 81.7 us -> 80.3 us
    pallas_call x1, Pallas kernels: 79.2 us -> 77.8 us  [run_exchange(): pl.pallas_call(exchange, out_shape=(jax.ShapeDtypeStruct((NBLK, ROWS, COL...]
where the time goes in v7:
time: 81.1 us; the launch traced here: 81 us
  Pallas kernels  80.3 us (99%)
    pallas_call x1, Pallas kernels, run_exchange(): pl.pallas_call(exchange, out_shape=(jax.ShapeDtypeStruct((NBLK, ROWS, COL...  77.8 us
    pallas_call x1, Pallas kernels, run_exchange(): pl.pallas_call(hand_over, out_shape=[jax.ShapeDtypeStruct(result.shape, r...  2.5 us

profile of v7, /device:TPU:1, one launch (start us, length us, event | category | flops | bytes accessed | tf_op | source)
XLA Modules:
  0.0 81.0 jit_solution(7558328427753636862)
XLA Ops:
  0.6 77.8 %shard_map.120 = (bf16[56,16,256]{2,1,0:T(8,128)(2,1)S(1)}, f32[56,16,256]{2,1,0:T(8,128)S(1)}, f32[2,256,1024]{2,1,0:T(8,128)S(1)}, f32[2,256,1024]{2,1,0:T(8,128)S(1)}) custom-call(s32[56]{0:T(128)} %slot_ref.1, s32[56]{0:T(128)} %rows_ref.1, s32[56]{0:T(128)} %cols_ref.1, bf16[56,16,256]{2,1,0:T(8,128)(2,1)} %grads_ref.1, f32[56,16,256]{2,1,0:T(8,128)} %second_ref.1, ...), custom_call_target="tpu_custom_call" | custom-call | flops 4294967296 | bytes 8388608 | tf_op jit(solution)/shard_map/pallas_call | solution.py:515
  78.5 2.5 %shard_map.121 = (bf16[56,16,256]{2,1,0:T(8,128)(2,1)}, f32[56,16,256]{2,1,0:T(8,128)}, f32[2,256,1024]{2,1,0:T(8,128)}, f32[2,256,1024]{2,1,0:T(8,128)}) custom-call(bf16[56,16,256]{2,1,0:T(8,128)(2,1)S(1)} %get-tuple-element.8.refs_0_, f32[56,16,256]{2,1,0:T(8,128)S(1)} %get-tuple-element.9.refs_1_, f32[2,256,1024]{2,1,0:T(8,128)S(1)} %get-tuple-element.10.refs_2_, ...), custom_call_target="tpu_custom_call" | custom-call | tf_op jit(solution)/shard_map/pallas_call | solution.py:579
